TPU v7x, 32 devices: a whole 2x2x4 slice. The times are simulated.
32 devices in a mesh: groups: 2 (over y), virt: 4 (over z), pair: 2 (over x), sub: 2 (over core).
Axes of the slice: x: 2, y: 2, z: 4, core: 2. Of those that a mesh axis runs over, the one named last changes fastest.
Arguments:
- amplitudes: bfloat16 [3840, 2048], P(('groups', 'pair', 'virt'), 'sub'), parts along dimension 0, may hold values from -4 to 4
- driver: bfloat16 [3840, 2048], P(('groups', 'pair', 'virt'), 'sub'), parts along dimension 0, may hold values from -6 to 6
- integrals: bfloat16 [4096, 2048], P(('groups', 'sub'), 'virt'), parts along dimension 0, may hold values from -0.125 to 0.125
- pair_energy: float32 [3840], P(('groups', 'pair', 'virt')), parts along dimension 0, may hold values from -1.5 to -0.5
- col_energy: float32 [4096], P(('groups', 'sub')), parts along dimension 0, may hold values from 0.5 to 3
- tile_irrep: int32 [32], P(('groups', 'sub')), parts along dimension 0, may hold values from 0 to 3
- pair_irrep: int32 [3840], P(('groups', 'pair', 'virt')), parts along dimension 0, may hold values from 0 to 3, as said below
- mirror_slot: int32 [3840], P(('groups', 'pair', 'virt')), parts along dimension 0, may hold values from 0 to 239, as said below
Outputs:
- amplitudes_next: float32 [3840, 2048], P(('groups', 'pair', 'virt'), 'sub'), parts along dimension 0
There are 2 independent parts, one for each index of `groups`. A program takes and returns all parts, laid end to end along the dimension named above; each array names one. Nothing has to cross between parts.
Inputs may be any that keep to these rules, and one draw needn't show every extreme that they name: `mirror_slot`: within each pair of mirrored blocks (block b and block b + 4) the map is a permutation whose entries point back to each other. `pair_irrep`: A pair and its mirror carry the same label.
All inputs are finite; a program needn't handle non-finite values.
Results may differ from a plain program's by a relative error of at most 0.00088.
Values may be sent and summed in bfloat16 or wider, within the bound.
No kernel may reach another device: no remote copies, remote signals or barrier semaphores. Data moves between devices by JAX's collectives and lax.ppermute only.
A program may use at most 64 MiB of HBM per device.

v0:
```python
import jax
import jax.numpy as jnp
from jax import lax
from jax.sharding import PartitionSpec as P

ITERS = 2


def from_partner(value, axis, apart):
    return lax.ppermute(value, axis, [(i, i ^ 1 << apart) for i in range(lax.axis_size(axis))])


def contract(blocks, integrals):
    total = jnp.dot(
        blocks[0],
        lax.all_gather(integrals, "virt", axis=1, tiled=True),
        preferred_element_type=jnp.float32,
    )
    return lax.psum_scatter(total, "sub", scatter_dimension=1, tiled=True)


def body(
    amplitudes, driver, integrals, pair_energy, col_energy, tile_irrep, pair_irrep, mirror_slot
):
    col_irrep = jnp.repeat(tile_irrep, 128)
    occupied = pair_irrep[:, None] == col_irrep[None, :]
    energy_gap = col_energy[None, :] - pair_energy[:, None]
    driver_wide = driver.astype(jnp.float32)
    partner_bit = lax.axis_size("pair").bit_length() - 2
    current = jnp.where(occupied, amplitudes, jnp.zeros((), amplitudes.dtype))
    updated = driver_wide
    for iteration in range(ITERS):
        ladder = contract((current,), integrals)
        mirror_block = from_partner(ladder, "pair", partner_bit)
        symmetric = ladder + jnp.take(mirror_block, mirror_slot, axis=0)
        updated = jnp.where(
            occupied, (driver_wide + symmetric) / energy_gap, jnp.zeros((), jnp.float32)
        )
        current = updated.astype(jnp.bfloat16)
    return updated


def solution(mesh):
    return jax.shard_map(
        body,
        mesh=mesh,
        in_specs=(
            P(("groups", "pair", "virt"), "sub"),
            P(("groups", "pair", "virt"), "sub"),
            P(("groups", "sub"), "virt"),
            P(("groups", "pair", "virt")),
            P(("groups", "sub")),
            P(("groups", "sub")),
            P(("groups", "pair", "virt")),
            P(("groups", "pair", "virt")),
        ),
        out_specs=P(("groups", "pair", "virt"), "sub"),
        check_vma=False,
    )
```

profile of v0, /device:TPU:0, one launch (start us, length us, event | category | flops | bytes accessed | tf_op | source)
XLA Modules:
  0.0 179.7 jit_solution(7452806266645492408)
XLA Ops:
  6.5 0.0 copy-start
  6.5 0.0 all-gather.2.cloned.1.call-start
  6.5 0.7 all-gather.2.cloned.1.call-update
  7.3 0.0 reduce-scatter.3.cloned.1.call-start
  7.3 0.0 copy-done
  7.3 0.1 broadcast_bitcast_fusion
  7.4 85.0 %all-gather.2.cloned.1.call-done = bf16[1024,2048]{1,0:T(8,128)(2,1)} async-done(((bf16[1024,512]{1,0:T(8,128)(2,1)}), bf16[1024,2048]{1,0:T(8,128)(2,1)}) %all-gather.2.cloned.1.call-update) | async-done | bytes 4194320 | tf_op jit(solution)/shard_map/all_gather | solution.py:16
  92.4 4.9 %fusion.3 = f32[240,2048]{1,0:T(8,128)} fusion(bf16[1024,2048]{1,0:T(8,128)(2,1)} %all-gather.2.cloned.1.call-done, bf16[240,1024]{1,0:T(8,128)(2,1)} %param.10, s32[1024]{0:T(1024)S(1)} %broadcast_bitcast_fusion, s32[240]{0:T(256)} %param.16), kind=kOutput, calls=%fused_computation.13 | convolution fusion | flops 1007124480 | bytes 6656960 | tf_op jit(solution)/shard_map/dot_general | solution.py:14
  97.3 0.0 reduce-scatter.3.cloned.1.call-update
  97.3 0.0 reduce-scatter.5.cloned.1.call-start
  97.4 8.1 %reduce-scatter.3.cloned.1.call-done = f32[240,1024]{1,0:T(8,128)} async-done(((f32[240,2048]{1,0:T(8,128)}), f32[240,1024]{1,0:T(8,128)}) %reduce-scatter.3.cloned.1.call-update) | async-done | bytes 983056 | tf_op jit(solution)/shard_map/reduce_scatter | solution.py:19
  105.5 1.7 collective-permute-start
  107.2 0.0 copy-done.6
  107.3 0.0 copy-start.2
  107.3 0.0 copy-start.3
  107.3 0.0 copy-start.4
  107.3 0.0 copy-start.5
  107.3 22.3 %collective-permute-done = f32[240,1024]{1,0:T(8,128)S(1)} collective-permute-done((f32[240,1024]{1,0:T(8,128)}, f32[240,1024]{1,0:T(8,128)S(1)}, u32[]{:S(2)}, u32[]{:S(2)}) %collective-permute-start) | collective-permute-done | bytes 983072 | tf_op jit(solution)/shard_map/ppermute | solution.py:10
  129.7 1.0 gather_fusion
  130.7 0.0 copy-done.2
  130.7 0.0 copy-done.3
  130.7 0.0 copy-done.4
  130.7 0.0 copy-done.5
  130.7 0.0 copy-done.7
  130.8 4.9 %fusion.1 = f32[240,2048]{1,0:T(8,128)} fusion(bf16[1024,2048]{1,0:T(8,128)(2,1)} %all-gather.2.cloned.1.call-done, f32[240,1024]{1,0:T(8,128)S(1)} %copy-done.7, f32[240,1024]{1,0:T(8,128)S(1)} %gather_fusion, bf16[240,1024]{1,0:T(8,128)(2,1)S(1)} %copy-done.2, f32[240]{0:T(256)S(1)} %copy-done.5, f32[1024]{0:T(1024)S(1)} %copy-done.4, ...), kind=kOutput, calls=%fused_computation.12 | convolution fusion | flops 1008844800 | bytes 8628336 | tf_op jit(solution)/shard_map/dot_general | solution.py:14
  135.7 0.0 reduce-scatter.5.cloned.1.call-update
  135.7 10.8 %reduce-scatter.5.cloned.1.call-done = f32[240,1024]{1,0:T(8,128)} async-done(((f32[240,2048]{1,0:T(8,128)}), f32[240,1024]{1,0:T(8,128)}) %reduce-scatter.5.cloned.1.call-update) | async-done | bytes 983056 | tf_op jit(solution)/shard_map/reduce_scatter | solution.py:19
  146.5 1.7 collective-permute-start.1
  148.3 22.5 %collective-permute-done.1 = f32[240,1024]{1,0:T(8,128)S(1)} collective-permute-done((f32[240,1024]{1,0:T(8,128)}, f32[240,1024]{1,0:T(8,128)S(1)}, u32[]{:S(2)}, u32[]{:S(2)}) %collective-permute-start.1) | collective-permute-done | bytes 983072 | tf_op jit(solution)/shard_map/ppermute | solution.py:10
  170.8 1.0 gather_fusion.1
  171.8 0.0 copy-done.1
  171.8 1.4 compare_select_fusion
  (6 shorter events, 0.0 us)
Async XLA Ops:
  6.5 0.8 copy-start
  6.5 85.9 %all-gather.2.cloned.1.call-start = ((), (), s32[]{:S(2)}) async-start(), calls=%async_computation.2 | async-start | bytes 5242880 | tf_op jit(solution)/shard_map/all_gather | solution.py:16
  7.3 98.3 %reduce-scatter.3.cloned.1.call-start = ((), (), s32[]{:S(2)}) async-start(), calls=%async_computation.3 | async-start | bytes 2949120 | tf_op jit(solution)/shard_map/reduce_scatter | solution.py:19
  7.4 99.9 %copy-start.6 = (s32[240]{0:T(256)S(1)}, s32[240]{0:T(256)}, u32[]{:S(2)}) copy-start(s32[240]{0:T(256)} %param.17) | copy-start | bytes 2884
  97.3 49.2 %reduce-scatter.5.cloned.1.call-start = ((), (), s32[]{:S(2)}) async-start(), calls=%async_computation.4 | async-start | bytes 2949120 | tf_op jit(solution)/shard_map/reduce_scatter | solution.py:19
  105.5 24.1 %collective-permute-start = (f32[240,1024]{1,0:T(8,128)}, f32[240,1024]{1,0:T(8,128)S(1)}, u32[]{:S(2)}, u32[]{:S(2)}) collective-permute-start(f32[240,1024]{1,0:T(8,128)} %reduce-scatter.3.cloned.1.call-done), channel_id=1, source_target_pairs={{0,2},{2,0},{1,3},{3,1},{4,6},{6,4},{5,7},{7,5},{8,10},{10,8},{9,1... | collective-permute-start | bytes 2949128 | tf_op jit(solution)/shard_map/ppermute | solution.py:10
  107.3 23.4 %copy-start.2 = (bf16[240,1024]{1,0:T(8,128)(2,1)S(1)}, bf16[240,1024]{1,0:T(8,128)(2,1)}, u32[]{:S(2)}) copy-start(bf16[240,1024]{1,0:T(8,128)(2,1)} %param.11) | copy-start | bytes 1474564
  107.3 23.4 %copy-start.3 = (s32[240]{0:T(256)S(1)}, s32[240]{0:T(256)}, u32[]{:S(2)}) copy-start(s32[240]{0:T(256)} %param.16) | copy-start | bytes 2884
  107.3 23.4 %copy-start.4 = (f32[1024]{0:T(1024)S(1)}, f32[1024]{0:T(1024)}, u32[]{:S(2)}) copy-start(f32[1024]{0:T(1024)} %param.14) | copy-start | bytes 12292
  107.3 23.4 %copy-start.5 = (f32[240]{0:T(256)S(1)}, f32[240]{0:T(256)}, u32[]{:S(2)}) copy-start(f32[240]{0:T(256)} %param.13) | copy-start | bytes 2884
  107.3 23.4 %copy-start.7 = (f32[240,1024]{1,0:T(8,128)S(1)}, f32[240,1024]{1,0:T(8,128)}, u32[]{:S(2)}) copy-start(f32[240,1024]{1,0:T(8,128)} %reduce-scatter.3.cloned.1.call-done) | copy-start | bytes 2949124
  146.5 25.3 %copy-start.1 = (f32[240,1024]{1,0:T(8,128)S(1)}, f32[240,1024]{1,0:T(8,128)}, u32[]{:S(2)}) copy-start(f32[240,1024]{1,0:T(8,128)} %reduce-scatter.5.cloned.1.call-done) | copy-start | bytes 2949124
  146.5 24.2 %collective-permute-start.1 = (f32[240,1024]{1,0:T(8,128)}, f32[240,1024]{1,0:T(8,128)S(1)}, u32[]{:S(2)}, u32[]{:S(2)}) collective-permute-start(f32[240,1024]{1,0:T(8,128)} %reduce-scatter.5.cloned.1.call-done), channel_id=1, source_target_pairs={{0,2},{2,0},{1,3},{3,1},{4,6},{6,4},{5,7},{7,5},{8,10},{10,8},{9,1... | collective-permute-start | bytes 2949128 | tf_op jit(solution)/shard_map/ppermute | solution.py:10
Sparse Core Ops, SparseCore 0:
  8.9 83.4 all-gather.1
  97.5 8.0 reduce-scatter.2
  135.8 10.6 reduce-scatter.4
where the time goes:
time: 180 us
  waiting for transfers between devices  150 us (83%)
  between operations  13.2 us (7%)
  matrix products  9.83 us (5%)
  starting transfers between devices  3.53 us (2%)
  local copies, waits for them, and re-layouts  2.18 us (1%)
    all_gather x1, waiting for transfers between devices, contract(): lax.all_gather(integrals, 'virt', axis=1, tiled=True)  85 us
    ppermute x2, waiting for transfers between devices, from_partner(): lax.ppermute(value, axis, [(i, i ^ 1 << apart) for i in range(lax.axis_si...  44.9 us
    reduce_scatter x2, waiting for transfers between devices, contract(): return lax.psum_scatter(total, 'sub', scatter_dimension=1, tiled=True)  18.9 us
    dot_general x2, matrix products, contract(): jnp.dot(blocks[0], lax.all_gather(integrals, 'virt', axis=1, tiled=True),...  9.83 us
  transfers between devices with their start and end apart: 5, of which 5 were waited for; matrix products, arithmetic and copies ran while one was open for 0% of the time, Pallas kernels for 0%

commit v1 on v0

--- a/solution.py
+++ b/solution.py
@@ -1,9 +1,15 @@
+import functools
+
 import jax
 import jax.numpy as jnp
 from jax import lax
+from jax.experimental import pallas as pl
+from jax.experimental.pallas import tpu as pltpu
 from jax.sharding import PartitionSpec as P
 
 ITERS = 2
+TILE = 128
+VMEM_BYTES = 48 * 1024 * 1024
 
 
 def from_partner(value, axis, apart):
@@ -19,10 +25,10 @@
     return lax.psum_scatter(total, "sub", scatter_dimension=1, tiled=True)
 
 
-def body(
+def dense_plan(
     amplitudes, driver, integrals, pair_energy, col_energy, tile_irrep, pair_irrep, mirror_slot
 ):
-    col_irrep = jnp.repeat(tile_irrep, 128)
+    col_irrep = jnp.repeat(tile_irrep, TILE)
     occupied = pair_irrep[:, None] == col_irrep[None, :]
     energy_gap = col_energy[None, :] - pair_energy[:, None]
     driver_wide = driver.astype(jnp.float32)
@@ -38,6 +44,292 @@
         )
         current = updated.astype(jnp.bfloat16)
     return updated
+
+
+class Plan:
+    def __init__(self, tiles, slab_tiles, places):
+        self.tiles = tiles
+        self.half = tiles // 2
+        self.slab = slab_tiles
+        self.places = places
+        self.cap = 8 * slab_tiles
+        self.shared = self.cap * 7 // 16
+        self.direct = self.cap - 2 * self.shared
+
+
+def label_of(own, other, sub, tile, half):
+    place = lax.rem(tile, half)
+    mine = (tile // half) == sub
+    return jnp.where(mine, own[place], other[place])
+
+
+def listed(plan, own, other, sub, slab, use):
+    def step(i, count):
+        j, k = i // plan.tiles, lax.rem(i, plan.tiles)
+        here = label_of(own, other, sub, slab * plan.slab + j, plan.half)
+        match = label_of(own, other, sub, k, plan.half) == here
+
+        @pl.when(match & (count < plan.cap))
+        def _():
+            use(count, k, j)
+
+        return count + match.astype(jnp.int32)
+
+    return lax.fori_loop(0, plan.slab * plan.tiles, step, jnp.int32(0))
+
+
+def tile_at(index):
+    return pl.ds(pl.multiple_of(index * TILE, TILE), TILE)
+
+
+def pack_kernel(plan, own, other, place, mine_ref, their_ref, shared_ref, direct_ref):
+    slab, side, sub = place[0], place[1], place[2]
+
+    def use(count, k, j):
+        def copy(to_ref, slot):
+            rows, cols = tile_at(lax.rem(k, plan.half)), tile_at(j)
+
+            @pl.when((k // plan.half) == sub)
+            def _():
+                to_ref[tile_at(slot), :] = mine_ref[rows, cols]
+
+            @pl.when((k // plan.half) != sub)
+            def _():
+                to_ref[tile_at(slot), :] = their_ref[rows, cols]
+
+        slot = count - side * plan.shared
+
+        @pl.when((slot >= 0) & (slot < plan.shared))
+        def _():
+            copy(shared_ref, slot)
+
+        @pl.when(count >= 2 * plan.shared)
+        def _():
+            copy(direct_ref, count - 2 * plan.shared)
+
+    shared_ref[...] = jnp.zeros_like(shared_ref)
+    direct_ref[...] = jnp.zeros_like(direct_ref)
+    listed(plan, own, other, sub, slab, use)
+
+
+def update(rows, cols, sym, driver, gap_own, occupied):
+    return jnp.where(occupied, (driver + sym) / gap_own, 0.0)
+
+
+def first_kernel(plan, rounds, *refs):
+    own, other, place, mine_ref, their_ref = refs[:5]
+    parts = refs[5 : 5 + 3 * rounds]
+    (cur_mine, cur_their, drv_own, drv_par, lab_row, pe_own, pe_par, col_energy) = refs[
+        5 + 3 * rounds : 13 + 3 * rounds
+    ]
+    ints_ref, cur_ref = refs[13 + 3 * rounds :]
+    z, side, sub = place[0], place[1], place[2]
+    half_places = plan.places // 2
+    width = plan.slab * TILE
+    rows_half = plan.half * TILE
+    ints_ref[...] = jnp.zeros_like(ints_ref)
+
+    def fill(slab, rs, xs, us):
+        first = (slab - sub * half_places) * plan.slab
+
+        def use(count, k, j):
+            rows, cols = tile_at(k), tile_at(first + j)
+
+            def copy(from_ref, slot):
+                ints_ref[rows, cols] = from_ref[tile_at(slot), :]
+
+            in_first = count < plan.shared
+            in_second = (count >= plan.shared) & (count < 2 * plan.shared)
+            from_here = (in_first & (side == 0)) | (in_second & (side == 1))
+            slot = jnp.where(in_first, count, count - plan.shared)
+
+            @pl.when(from_here)
+            def _():
+                copy(rs, slot)
+
+            @pl.when((in_first | in_second) & jnp.logical_not(from_here))
+            def _():
+                copy(xs, slot)
+
+            @pl.when(count >= 2 * plan.shared)
+            def _():
+                copy(us, count - 2 * plan.shared)
+
+        listed(plan, own, other, sub, slab, use)
+
+    for r in range(1, rounds):
+        slab = lax.rem(z - r + plan.places, plan.places)
+        slab = jnp.where(
+            slab // half_places == sub, slab, lax.rem(slab + half_places, plan.places)
+        )
+        fill(slab, *parts[3 * r : 3 * r + 3])
+
+    @pl.when(z // half_places == sub)
+    def _():
+        cols = pl.ds(pl.multiple_of((z - sub * half_places) * width, TILE), width)
+        mine_at = pl.ds(pl.multiple_of(sub * rows_half, TILE), rows_half)
+        their_at = pl.ds(pl.multiple_of((1 - sub) * rows_half, TILE), rows_half)
+        ints_ref[mine_at, cols] = mine_ref[...]
+        ints_ref[their_at, cols] = their_ref[...]
+
+    @pl.when(z // half_places != sub)
+    def _():
+        fill(lax.rem(z + half_places, plan.places), *parts[:3])
+
+    multiply(
+        plan, own, place, cur_mine, cur_their, ints_ref, drv_own, drv_par, lab_row, pe_own, pe_par,
+        col_energy, cur_ref,
+    )
+
+
+def multiply(
+    plan, own, place, cur_mine, cur_their, ints_ref, drv_own, drv_par, lab_row, pe_own, pe_par,
+    col_energy, out_ref,
+):
+    sub = place[2]
+    rows_half = plan.half * TILE
+    mine_at = pl.ds(pl.multiple_of(sub * rows_half, TILE), rows_half)
+    their_at = pl.ds(pl.multiple_of((1 - sub) * rows_half, TILE), rows_half)
+    rows = drv_own.shape[0]
+    wide = 2 * TILE
+
+    def block(c, _):
+        cols = pl.ds(pl.multiple_of(c * wide, wide), wide)
+        total = jnp.dot(
+            cur_mine[...], ints_ref[mine_at, cols], preferred_element_type=jnp.float32
+        ) + jnp.dot(cur_their[...], ints_ref[their_at, cols], preferred_element_type=jnp.float32)
+        sym = total[:rows] + total[rows:]
+        for t in range(2):
+            at = pl.ds(pl.multiple_of(c * wide + t * TILE, TILE), TILE)
+            part = sym[:, t * TILE : (t + 1) * TILE]
+            occupied = lab_row[...] == own[2 * c + t]
+            energy = col_energy[:, at]
+            new = jnp.where(
+                occupied, (drv_own[:, at].astype(jnp.float32) + part) / (energy - pe_own[...]), 0.0
+            )
+            out_ref[:rows, at] = new.astype(out_ref.dtype)
+            if out_ref.shape[0] > rows:
+                new = jnp.where(
+                    occupied,
+                    (drv_par[:, at].astype(jnp.float32) + part) / (energy - pe_par[...]),
+                    0.0,
+                )
+                out_ref[rows:, at] = new.astype(out_ref.dtype)
+        return 0
+
+    lax.fori_loop(0, plan.half // 2, block, 0)
+
+
+def second_kernel(plan, own, place, cur_mine, cur_their, ints_ref, drv_own, lab_row, pe_own,
+                  col_energy, out_ref):
+    multiply(
+        plan, own, place, cur_mine, cur_their, ints_ref, drv_own, None, lab_row, pe_own, None,
+        col_energy, out_ref,
+    )
+
+
+def in_smem(count):
+    return [pl.BlockSpec(memory_space=pltpu.SMEM)] * count
+
+
+def in_vmem(count):
+    return [pl.BlockSpec(memory_space=pltpu.VMEM)] * count
+
+
+def call(kernel, smem, vmem, outs, flops=0):
+    moved = sum(v.size * v.dtype.itemsize for v in vmem)
+    single = not isinstance(outs, (list, tuple))
+    return pl.pallas_call(
+        kernel,
+        out_shape=outs,
+        in_specs=in_smem(len(smem)) + in_vmem(len(vmem)),
+        out_specs=in_vmem(1)[0] if single else in_vmem(len(outs)),
+        compiler_params=pltpu.CompilerParams(vmem_limit_bytes=VMEM_BYTES),
+        cost_estimate=pl.CostEstimate(flops=flops, bytes_accessed=2 * moved, transcendentals=0),
+    )(*smem, *vmem)
+
+
+def body(
+    amplitudes, driver, integrals, pair_energy, col_energy, tile_irrep, pair_irrep, mirror_slot
+):
+    places, sides = lax.axis_size("virt"), lax.axis_size("pair")
+    partner_bit = sides.bit_length() - 2
+    rows, half_cols = amplitudes.shape
+    plan = Plan(2 * half_cols // TILE, integrals.shape[1] // TILE, places)
+    half_places = places // 2
+    z, sub = lax.axis_index("virt"), lax.axis_index("sub")
+    side = (lax.axis_index("pair") >> partner_bit) & 1
+    place = jnp.stack([z, side, sub]).astype(jnp.int32)
+
+    other_irrep = from_partner(tile_irrep, "sub", 0)
+    their_ints = from_partner(integrals, "sub", 0)
+
+    occupied = pair_irrep[:, None] == jnp.repeat(tile_irrep, TILE)[None, :]
+    masked = jnp.where(occupied, amplitudes, jnp.zeros((), amplitudes.dtype))
+    mirror_amps = jnp.take(from_partner(masked, "pair", partner_bit), mirror_slot, axis=0)
+    mirror_drv = jnp.take(from_partner(driver, "pair", partner_bit), mirror_slot, axis=0)
+    mirror_energy = jnp.take(from_partner(pair_energy, "pair", partner_bit), mirror_slot, axis=0)
+    cur_mine = jnp.concatenate([masked, mirror_amps], axis=0)
+    cur_their = from_partner(cur_mine, "sub", 0)
+
+    tile = jax.ShapeDtypeStruct((TILE, TILE), integrals.dtype)
+    shared, direct = call(
+        functools.partial(pack_kernel, plan),
+        (tile_irrep, other_irrep, place),
+        (integrals, their_ints),
+        [
+            jax.ShapeDtypeStruct((plan.shared * TILE, TILE), tile.dtype),
+            jax.ShapeDtypeStruct((plan.direct * TILE, TILE), tile.dtype),
+        ],
+    )
+    parts = []
+    for r in range(half_places):
+        pairs = []
+        for i in range(places):
+            for core in range(2):
+                to = (i + r + half_places * (1 - core)) % places
+                if to != i:
+                    pairs.append((2 * i + core, 2 * to + i // half_places))
+        got_shared = lax.ppermute(shared, ("virt", "sub"), pairs)
+        got_direct = lax.ppermute(direct, ("virt", "sub"), pairs)
+        parts += [got_shared, from_partner(got_shared, "pair", partner_bit), got_direct]
+
+    lab_row = pair_irrep[:, None]
+    pe_own, pe_par = pair_energy[:, None], mirror_energy[:, None]
+    energy = col_energy[None, :]
+    flops = 2 * 2 * rows * plan.tiles * TILE * half_cols
+    ints, cur_mine = call(
+        functools.partial(first_kernel, plan, half_places),
+        (tile_irrep, other_irrep, place),
+        (integrals, their_ints, *parts, cur_mine, cur_their, driver, mirror_drv, lab_row, pe_own,
+         pe_par, energy),
+        [
+            jax.ShapeDtypeStruct((plan.tiles * TILE, half_cols), integrals.dtype),
+            jax.ShapeDtypeStruct((2 * rows, half_cols), integrals.dtype),
+        ],
+        flops,
+    )
+    cur_their = from_partner(cur_mine, "sub", 0)
+
+    def sparse_end():
+        return call(
+            functools.partial(second_kernel, plan),
+            (tile_irrep, place),
+            (cur_mine, cur_their, ints, driver, lab_row, pe_own, energy),
+            jax.ShapeDtypeStruct((rows, half_cols), jnp.float32),
+            flops,
+        )
+
+    def dense_end():
+        return dense_plan(
+            amplitudes, driver, integrals, pair_energy, col_energy, tile_irrep, pair_irrep,
+            mirror_slot,
+        )
+
+    labels = jnp.concatenate([tile_irrep, other_irrep])
+    by_slab = jnp.where(sub == 0, labels, jnp.roll(labels, plan.half))
+    needed = (by_slab[:, None] == labels[None, :]).sum(axis=1).reshape(places, plan.slab).sum(axis=1)
+    return lax.cond((needed > plan.cap).any(), dense_end, sparse_end)
 
 
 def solution(mesh):

time: 180 us -> 108 us (0.60)
  waiting for transfers between devices: 150 us -> 33.6 us
  starting transfers between devices: 3.53 us -> 25.2 us
  Pallas kernels: 0 us -> 19.3 us
  matrix products: 9.83 us -> 0 us
  local copies, waits for them, and re-layouts: 2.18 us -> 11.3 us
  other arithmetic: 1.37 us -> 3.98 us
    all_gather x1 -> x0, waiting for transfers between devices: 85 us -> none  [contract(): lax.all_gather(integrals, 'virt', axis=1, tiled=True)]
    ppermute x2 -> x9, waiting for transfers between devices: 44.9 us -> 22.6 us  [from_partner(): lax.ppermute(value, axis, [(i, i ^ 1 << apart) for i in range(lax.axis_si...]
    pallas_call x0 -> x3, Pallas kernels: none -> 19.3 us  [call(): pl.pallas_call(kernel, out_shape=outs, in_specs=in_smem(len(smem)) + in_v...]
    reduce_scatter x2 -> x0, waiting for transfers between devices: 18.9 us -> none  [contract(): return lax.psum_scatter(total, 'sub', scatter_dimension=1, tiled=True)]
    ppermute x0 -> x4, starting transfers between devices: none -> 17.2 us  [the longest x2 11.4 us: body(): got_direct = lax.ppermute(direct, ('virt', 'sub'), pairs)]
    ppermute x0 -> x4, waiting for transfers between devices: none -> 11.1 us  [the longest x2 11.1 us: body(): got_shared = lax.ppermute(shared, ('virt', 'sub'), pairs)]
    dot_general x2 -> x0, matrix products: 9.83 us -> none  [contract(): jnp.dot(blocks[0], lax.all_gather(integrals, 'virt', axis=1, tiled=True),...]
    ppermute x2 -> x9, starting transfers between devices: 3.44 us -> 7.99 us  [from_partner(): lax.ppermute(value, axis, [(i, i ^ 1 << apart) for i in range(lax.axis_si...]
  transfers between devices with their start and end apart: 5 -> 13, of which waited for: 5 -> 6; matrix products, arithmetic and copies ran while one was open for 0% -> 11% of each run, Pallas kernels for 0% -> 4%
where the time goes in v1:
time: 108 us
  waiting for transfers between devices  33.6 us (31%)
  starting transfers between devices  25.2 us (23%)
  Pallas kernels  19.3 us (18%)
  between operations  14.2 us (13%)
  local copies, waits for them, and re-layouts  11.3 us (10%)
  other arithmetic  3.98 us (4%)
    ppermute x9, waiting for transfers between devices, from_partner(): lax.ppermute(value, axis, [(i, i ^ 1 << apart) for i in range(lax.axis_si...  22.6 us
    pallas_call x3, Pallas kernels, call(): pl.pallas_call(kernel, out_shape=outs, in_specs=in_smem(len(smem)) + in_v...  19.3 us
    ppermute x2, starting transfers between devices, body(): got_direct = lax.ppermute(direct, ('virt', 'sub'), pairs)  11.4 us
    ppermute x2, waiting for transfers between devices, body(): got_shared = lax.ppermute(shared, ('virt', 'sub'), pairs)  11.1 us
    ppermute x9, starting transfers between devices, from_partner(): lax.ppermute(value, axis, [(i, i ^ 1 << apart) for i in range(lax.axis_si...  7.99 us
    ppermute x2, starting transfers between devices, body(): got_shared = lax.ppermute(shared, ('virt', 'sub'), pairs)  5.79 us
    unnamed x18, local copies, waits for them, and re-layouts  3.67 us
  transfers between devices with their start and end apart: 13, of which 6 were waited for; matrix products, arithmetic and copies ran while one was open for 11% of the time, Pallas kernels for 4%

profile of v1, /device:TPU:0, one launch (start us, length us, event | category | flops | bytes accessed | tf_op | source)
XLA Modules:
  0.0 107.7 jit_solution(6146808736025728103)
XLA Ops:
  7.0 2.5 %collective-permute-start.13 = (f32[240]{0:T(256)}, f32[240]{0:T(256)S(1)}, u32[]{:S(2)}, u32[]{:S(2)}) collective-permute-start(f32[240]{0:T(256)} %param.17), channel_id=1, source_target_pairs={{0,2},{2,0},{1,3},{3,1},{4,6},{6,4},{5,7},{7,5},{8,10},{10,8},{9,1... | collective-permute-start | bytes 2888 | tf_op jit(solution)/shard_map/ppermute | solution.py:16
  9.5 0.7 broadcast_bitcast_fusion.1
  10.2 1.2 %compare_select_fusion.5 = bf16[240,1024]{1,0:T(8,128)(2,1)S(1)} fusion(bf16[240,1024]{1,0:T(8,128)(2,1)} %param.14, s32[1024]{0:T(1024)S(1)} %broadcast_bitcast_fusion.1, s32[240]{0:T(256)} %param.20), kind=kLoop, calls=%fused_computation.35 | loop fusion | flops 491520 | bytes 988096 | tf_op jit(solution)/shard_map/jit(_where)/select_n | solution.py:268
  11.5 2.0 %collective-permute-start.12 = (bf16[240,1024]{1,0:T(8,128)(2,1)}, bf16[240,1024]{1,0:T(8,128)(2,1)S(1)}, u32[]{:S(2)}, u32[]{:S(2)}) collective-permute-start(bf16[240,1024]{1,0:T(8,128)(2,1)} %refs_13_.1), channel_id=1, source_target_pairs={{0,2},{2,0},{1,3},{3,1},{4,6},{6,4},{5,7},{7,5},{8,10},{10,8},{9,1... | collective-permute-start | bytes 1474568 | tf_op jit(solution)/shard_map/ppermute | solution.py:16
  13.5 0.7 compare_select_fusion.6
  14.2 1.9 %gather_fusion.2 = f32[240]{0:T(256)S(1)} fusion(f32[240]{0:T(256)S(1)} %collective-permute-done.13, s32[1024]{0:T(1024)S(1)} %pad_clamp_fusion.1), kind=kCustom, calls=%fused_computation.4 | custom fusion | bytes 2880 | tf_op jit(solution)/shard_map/jit(_take)/gather | solution.py:271
  16.2 0.7 broadcast_select_fusion.3
  16.8 8.7 %collective-permute-done.10 = bf16[240,1024]{1,0:T(8,128)(2,1)S(1)} collective-permute-done((bf16[240,1024]{1,0:T(8,128)(2,1)S(1)}, bf16[240,1024]{1,0:T(8,128)(2,1)S(1)}, u32[]{:S(2)}, u32[]{:S(2)}) %collective-permute-start.10) | collective-permute-done | bytes 491552 | tf_op jit(solution)/shard_map/ppermute | solution.py:16
  25.5 1.1 %gather_fusion.3 = bf16[240,1024]{1,0:T(8,128)(2,1)S(1)} fusion(bf16[240,1024]{1,0:T(8,128)(2,1)S(1)} %collective-permute-done.10, s32[1024]{0:T(1024)S(1)} %pad_clamp_fusion.1), kind=kCustom, calls=%fused_computation.clone | custom fusion | bytes 984000 | tf_op jit(solution)/shard_map/jit(_take)/gather | solution.py:269
  26.7 8.7 %collective-permute-done.12 = bf16[240,1024]{1,0:T(8,128)(2,1)S(1)} collective-permute-done((bf16[240,1024]{1,0:T(8,128)(2,1)}, bf16[240,1024]{1,0:T(8,128)(2,1)S(1)}, u32[]{:S(2)}, u32[]{:S(2)}) %collective-permute-start.12) | collective-permute-done | bytes 491552 | tf_op jit(solution)/shard_map/ppermute | solution.py:16
  35.4 1.1 %gather_fusion.4 = bf16[240,1024]{1,0:T(8,128)(2,1)S(1)} fusion(bf16[240,1024]{1,0:T(8,128)(2,1)S(1)} %collective-permute-done.12, s32[1024]{0:T(1024)S(1)} %pad_clamp_fusion.1), kind=kCustom, calls=%fused_computation.2.clone | custom fusion | bytes 984000 | tf_op jit(solution)/shard_map/jit(_take)/gather | solution.py:270
  36.9 4.1 %shard_map.84 = (bf16[1792,128]{1,0:T(8,128)(2,1)S(1)}, bf16[512,128]{1,0:T(8,128)(2,1)}) custom-call(s32[8]{0:T(128)S(1)} %copy-done.8, s32[8]{0:T(128)S(1)} %collective-permute-done.2.other.refs_1_, s32[3]{0:T(128)S(1)} %pad_add_fusion.1.place.refs_2_, bf16[1024,512]{1,0:T(8,128)(2,1)} %refs_3_.1, ...), custom_call_target="tpu_custom_call" | custom-call | bytes 4194304 | tf_op jit(solution)/shard_map/pallas_call | solution.py:242
  41.1 3.6 %collective-permute-start.7 = (bf16[1792,128]{1,0:T(8,128)(2,1)S(1)}, bf16[1792,128]{1,0:T(8,128)(2,1)}, u32[]{:S(2)}, u32[]{:S(2)}) collective-permute-start(bf16[1792,128]{1,0:T(8,128)(2,1)S(1)} %get-tuple-element.65), channel_id=1, source_target_pairs={{0,12},{1,4},{4,0},{5,8},{8,5},{9,13},{12,9},{13,1},{2,14},{3,6},{... | collective-permute-start | bytes 1376264 | tf_op jit(solution)/shard_map/ppermute | solution.py:293
  44.6 2.2 %collective-permute-start.4 = (bf16[1792,128]{1,0:T(8,128)(2,1)S(1)}, bf16[1792,128]{1,0:T(8,128)(2,1)}, u32[]{:S(2)}, u32[]{:S(2)}) collective-permute-start(bf16[1792,128]{1,0:T(8,128)(2,1)S(1)} %get-tuple-element.65), channel_id=1, source_target_pairs={{0,8},{4,12},{8,1},{12,5},{2,10},{6,14},{10,3},{14,7},{16,24},{20,... | collective-permute-start | bytes 1376264 | tf_op jit(solution)/shard_map/ppermute | solution.py:293
  46.9 7.1 %collective-permute-done.7.refs_8_ = bf16[1792,128]{1,0:T(8,128)(2,1)} collective-permute-done((bf16[1792,128]{1,0:T(8,128)(2,1)S(1)}, bf16[1792,128]{1,0:T(8,128)(2,1)}, u32[]{:S(2)}, u32[]{:S(2)}) %collective-permute-start.7) | collective-permute-done | bytes 458784 | tf_op jit(solution)/shard_map/ppermute | solution.py:293
  53.9 4.0 %collective-permute-done.4.refs_5_ = bf16[1792,128]{1,0:T(8,128)(2,1)} collective-permute-done((bf16[1792,128]{1,0:T(8,128)(2,1)S(1)}, bf16[1792,128]{1,0:T(8,128)(2,1)}, u32[]{:S(2)}, u32[]{:S(2)}) %collective-permute-start.4) | collective-permute-done | bytes 458784 | tf_op jit(solution)/shard_map/ppermute | solution.py:293
  58.3 9.5 %collective-permute-start.9 = (bf16[512,128]{1,0:T(8,128)(2,1)}, bf16[512,128]{1,0:T(8,128)(2,1)}, u32[]{:S(2)}, u32[]{:S(2)}) collective-permute-start(bf16[512,128]{1,0:T(8,128)(2,1)} %get-tuple-element.66), channel_id=1, source_target_pairs={{0,12},{1,4},{4,0},{5,8},{8,5},{9,13},{12,9},{13,1},{2,14},{3,6},{... | collective-permute-start | bytes 393224 | tf_op jit(solution)/shard_map/ppermute | solution.py:294
  67.8 1.9 %collective-permute-start.6 = (bf16[512,128]{1,0:T(8,128)(2,1)}, bf16[512,128]{1,0:T(8,128)(2,1)}, u32[]{:S(2)}, u32[]{:S(2)}) collective-permute-start(bf16[512,128]{1,0:T(8,128)(2,1)} %get-tuple-element.66), channel_id=1, source_target_pairs={{0,8},{4,12},{8,1},{12,5},{2,10},{6,14},{10,3},{14,7},{16,24},{20,... | collective-permute-start | bytes 393224 | tf_op jit(solution)/shard_map/ppermute | solution.py:294
  69.8 0.8 copy.16.refs_15_
  70.5 0.8 copy.17.refs_16_
  71.3 0.8 copy.18.refs_17_
  72.1 4.7 %collective-permute-done.5.refs_6_ = bf16[1792,128]{1,0:T(8,128)(2,1)} collective-permute-done((bf16[1792,128]{1,0:T(8,128)(2,1)}, bf16[1792,128]{1,0:T(8,128)(2,1)}, u32[]{:S(2)}, u32[]{:S(2)}) %collective-permute-start.5) | collective-permute-done | bytes 458784 | tf_op jit(solution)/shard_map/ppermute | solution.py:16
  76.8 0.9 copy-done
  77.7 0.9 copy-done.1
  78.6 0.9 copy-done.2
  79.5 9.7 %shard_map.85 = (bf16[2048,1024]{1,0:T(8,128)(2,1)}, bf16[480,1024]{1,0:T(8,128)(2,1)}) custom-call(s32[8]{0:T(128)S(1)} %copy-done.8, s32[8]{0:T(128)S(1)} %collective-permute-done.2.other.refs_1_, s32[3]{0:T(128)S(1)} %pad_add_fusion.1.place.refs_2_, bf16[1024,512]{1,0:T(8,128)(2,1)} %refs_3_.1, ...), custom_call_target="tpu_custom_call" | custom-call | flops 2013265920 | bytes 14300800 | tf_op jit(solution)/shard_map/pallas_call | solution.py:242
  89.2 2.5 %collective-permute-start.14 = (bf16[480,1024]{1,0:T(8,128)(2,1)}, bf16[480,1024]{1,0:T(8,128)(2,1)S(1)}, u32[]{:S(2)}, u32[]{:S(2)}) collective-permute-start(bf16[480,1024]{1,0:T(8,128)(2,1)} %get-tuple-element.67), channel_id=1, source_target_pairs={{0,1},{1,0},{2,3},{3,2},{4,5},{5,4},{6,7},{7,6},{8,9},{9,8},{10,11... | collective-permute-start | bytes 2949128 | tf_op jit(solution)/shard_map/ppermute | solution.py:16
  92.2 0.7 compare_reduce_fusion
  93.5 0.5 collective-permute-done.14
  94.1 5.8 %conditional.1 = (f32[240,1024]{1,0:T(8,128)S(1)}) conditional(s32[]{:T(128)} %convert_element_type.13, (s32[8]{0:T(128)S(1)}, s32[3]{0:T(128)S(1)}, bf16[480,1024]{1,0:T(8,128)(2,1)}, bf16[480,1024]{1,0:T(8,128)(2,1)S(1)}, bf16[2048,1024]{1,0:T(8,128)(2,1)}, /*index=5*/bf16[240,1024]{1,0:T(8,128)(2,1)}, s32[240,1]{0,1:T(1,128)S(1)}, ...), branch_computations={%region_3.5_spmd, %region_4.9_spmd} | conditional | flops 2017938560 | bytes 73801048 | solution.py:332
  94.4 5.5 %branch_0_fun.1 = f32[240,1024]{1,0:T(8,128)S(1)} custom-call(s32[8]{0:T(128)S(1)} %get-tuple-element.42.own, s32[3]{0:T(128)S(1)} %get-tuple-element.44.place, bf16[480,1024]{1,0:T(8,128)(2,1)} %get-tuple-element.46.cur_mine, bf16[480,1024]{1,0:T(8,128)(2,1)S(1)} %get-tuple-element.47.cur_their, bf16[2048,1024]{1,0:T(8,128)(2,1)} %get-tuple-element.48.ints_ref, ...), custom_call_target="tpu_custom_call" | custom-call | flops 2013265920 | bytes 13315840 | tf_op jit(solution)/shard_map/cond/branch_0_fun/pallas_call | solution.py:242
  99.9 0.9 copy-done.5
  (37 shorter events, 2.1 us)
Async XLA Ops:
  6.5 30.4 %collective-permute-start.2 = (s32[8]{0:T(128)}, s32[8]{0:T(128)S(1)}, u32[]{:S(2)}, u32[]{:S(2)}) collective-permute-start(s32[8]{0:T(128)} %refs_0_.1), channel_id=1, source_target_pairs={{0,1},{1,0},{2,3},{3,2},{4,5},{5,4},{6,7},{7,6},{8,9},{9,8},{10,11... | collective-permute-start | bytes 104 | tf_op jit(solution)/shard_map/ppermute | solution.py:16
  7.0 7.2 %collective-permute-start.13 = (f32[240]{0:T(256)}, f32[240]{0:T(256)S(1)}, u32[]{:S(2)}, u32[]{:S(2)}) collective-permute-start(f32[240]{0:T(256)} %param.17), channel_id=1, source_target_pairs={{0,2},{2,0},{1,3},{3,1},{4,6},{6,4},{5,7},{7,5},{8,10},{10,8},{9,1... | collective-permute-start | bytes 2888 | tf_op jit(solution)/shard_map/ppermute | solution.py:16
  11.4 14.1 %collective-permute-start.10 = (bf16[240,1024]{1,0:T(8,128)(2,1)S(1)}, bf16[240,1024]{1,0:T(8,128)(2,1)S(1)}, u32[]{:S(2)}, u32[]{:S(2)}) collective-permute-start(bf16[240,1024]{1,0:T(8,128)(2,1)S(1)} %compare_select_fusion.5), channel_id=1, source_target_pairs={{0,2},{2,0},{1,3},{3,1},{4,6},{6,4},{5,7},{7,5},{8,10},{10,8},{9,1... | collective-permute-start | bytes 1474568 | tf_op jit(solution)/shard_map/ppermute | solution.py:16
  11.5 23.9 %collective-permute-start.12 = (bf16[240,1024]{1,0:T(8,128)(2,1)}, bf16[240,1024]{1,0:T(8,128)(2,1)S(1)}, u32[]{:S(2)}, u32[]{:S(2)}) collective-permute-start(bf16[240,1024]{1,0:T(8,128)(2,1)} %refs_13_.1), channel_id=1, source_target_pairs={{0,2},{2,0},{1,3},{3,1},{4,6},{6,4},{5,7},{7,5},{8,10},{10,8},{9,1... | collective-permute-start | bytes 1474568 | tf_op jit(solution)/shard_map/ppermute | solution.py:16
  13.5 23.4 %collective-permute-start.3 = (bf16[1024,512]{1,0:T(8,128)(2,1)}, bf16[1024,512]{1,0:T(8,128)(2,1)S(1)}, u32[]{:S(2)}, u32[]{:S(2)}) collective-permute-start(bf16[1024,512]{1,0:T(8,128)(2,1)} %refs_3_.1), channel_id=1, source_target_pairs={{0,1},{1,0},{2,3},{3,2},{4,5},{5,4},{6,7},{7,6},{8,9},{9,8},{10,11... | collective-permute-start | bytes 3145736 | tf_op jit(solution)/shard_map/ppermute | solution.py:16
  26.7 10.2 %copy-start.8 = (s32[8]{0:T(128)S(1)}, s32[8]{0:T(128)}, u32[]{:S(2)}) copy-start(s32[8]{0:T(128)} %refs_0_.1) | copy-start | bytes 100
  26.7 43.1 %copy-start.7 = (s32[240]{0:T(256)S(1)}, s32[240]{0:T(256)}, u32[]{:S(2)}) copy-start(s32[240]{0:T(256)} %param.20) | copy-start | bytes 2884
  26.7 43.9 %copy-start.9 = (f32[240]{0:T(256)S(1)}, f32[240]{0:T(256)}, u32[]{:S(2)}) copy-start(f32[240]{0:T(256)} %param.17) | copy-start | bytes 2884
  36.5 40.3 %copy-start.6 = (f32[1024]{0:T(1024)S(1)}, f32[1024]{0:T(1024)}, u32[]{:S(2)}) copy-start(f32[1024]{0:T(1024)} %param.18) | copy-start | bytes 12292
  36.7 35.4 %collective-permute-start.11 = (bf16[480,1024]{1,0:T(8,128)(2,1)S(1)}, bf16[480,1024]{1,0:T(8,128)(2,1)S(1)}, u32[]{:S(2)}, u32[]{:S(2)}) collective-permute-start(bf16[480,1024]{1,0:T(8,128)(2,1)S(1)} %pad_maximum_fusion.refs_11_), channel_id=1, source_target_pairs={{0,1},{1,0},{2,3},{3,2},{4,5},{5,4},{6,7},{7,6},{8,9},{9,8},{10,11... | collective-permute-start | bytes 2949128 | tf_op jit(solution)/shard_map/ppermute | solution.py:16
  41.1 53.0 %copy-start.10 = (s32[240]{0:T(256)S(1)}, s32[240]{0:T(256)}, u32[]{:S(2)}) copy-start(s32[240]{0:T(256)} %param.21) | copy-start | bytes 2884
  41.1 12.9 %collective-permute-start.7 = (bf16[1792,128]{1,0:T(8,128)(2,1)S(1)}, bf16[1792,128]{1,0:T(8,128)(2,1)}, u32[]{:S(2)}, u32[]{:S(2)}) collective-permute-start(bf16[1792,128]{1,0:T(8,128)(2,1)S(1)} %get-tuple-element.65), channel_id=1, source_target_pairs={{0,12},{1,4},{4,0},{5,8},{8,5},{9,13},{12,9},{13,1},{2,14},{3,6},{... | collective-permute-start | bytes 1376264 | tf_op jit(solution)/shard_map/ppermute | solution.py:293
  44.6 13.3 %collective-permute-start.4 = (bf16[1792,128]{1,0:T(8,128)(2,1)S(1)}, bf16[1792,128]{1,0:T(8,128)(2,1)}, u32[]{:S(2)}, u32[]{:S(2)}) collective-permute-start(bf16[1792,128]{1,0:T(8,128)(2,1)S(1)} %get-tuple-element.65), channel_id=1, source_target_pairs={{0,8},{4,12},{8,1},{12,5},{2,10},{6,14},{10,3},{14,7},{16,24},{20,... | collective-permute-start | bytes 1376264 | tf_op jit(solution)/shard_map/ppermute | solution.py:293
  53.9 18.2 %collective-permute-start.8 = (bf16[1792,128]{1,0:T(8,128)(2,1)}, bf16[1792,128]{1,0:T(8,128)(2,1)}, u32[]{:S(2)}, u32[]{:S(2)}) collective-permute-start(bf16[1792,128]{1,0:T(8,128)(2,1)} %collective-permute-done.7.refs_8_), channel_id=1, source_target_pairs={{0,2},{2,0},{1,3},{3,1},{4,6},{6,4},{5,7},{7,5},{8,10},{10,8},{9,1... | collective-permute-start | bytes 1376264 | tf_op jit(solution)/shard_map/ppermute | solution.py:16
  57.9 18.9 %collective-permute-start.5 = (bf16[1792,128]{1,0:T(8,128)(2,1)}, bf16[1792,128]{1,0:T(8,128)(2,1)}, u32[]{:S(2)}, u32[]{:S(2)}) collective-permute-start(bf16[1792,128]{1,0:T(8,128)(2,1)} %collective-permute-done.4.refs_5_), channel_id=1, source_target_pairs={{0,2},{2,0},{1,3},{3,1},{4,6},{6,4},{5,7},{7,5},{8,10},{10,8},{9,1... | collective-permute-start | bytes 1376264 | tf_op jit(solution)/shard_map/ppermute | solution.py:16
  58.3 13.8 %collective-permute-start.9 = (bf16[512,128]{1,0:T(8,128)(2,1)}, bf16[512,128]{1,0:T(8,128)(2,1)}, u32[]{:S(2)}, u32[]{:S(2)}) collective-permute-start(bf16[512,128]{1,0:T(8,128)(2,1)} %get-tuple-element.66), channel_id=1, source_target_pairs={{0,12},{1,4},{4,0},{5,8},{8,5},{9,13},{12,9},{13,1},{2,14},{3,6},{... | collective-permute-start | bytes 393224 | tf_op jit(solution)/shard_map/ppermute | solution.py:294
  67.8 4.3 %collective-permute-start.6 = (bf16[512,128]{1,0:T(8,128)(2,1)}, bf16[512,128]{1,0:T(8,128)(2,1)}, u32[]{:S(2)}, u32[]{:S(2)}) collective-permute-start(bf16[512,128]{1,0:T(8,128)(2,1)} %get-tuple-element.66), channel_id=1, source_target_pairs={{0,8},{4,12},{8,1},{12,5},{2,10},{6,14},{10,3},{14,7},{16,24},{20,... | collective-permute-start | bytes 393224 | tf_op jit(solution)/shard_map/ppermute | solution.py:294
  76.8 0.9 copy-start
  77.7 0.9 copy-start.1
  78.6 0.9 copy-start.2
  89.2 4.9 %collective-permute-start.14 = (bf16[480,1024]{1,0:T(8,128)(2,1)}, bf16[480,1024]{1,0:T(8,128)(2,1)S(1)}, u32[]{:S(2)}, u32[]{:S(2)}) collective-permute-start(bf16[480,1024]{1,0:T(8,128)(2,1)} %get-tuple-element.67), channel_id=1, source_target_pairs={{0,1},{1,0},{2,3},{3,2},{4,5},{5,4},{6,7},{7,6},{8,9},{9,8},{10,11... | collective-permute-start | bytes 2949128 | tf_op jit(solution)/shard_map/ppermute | solution.py:16
  99.9 0.9 copy-start.5

commit v2 on v0

--- a/solution.py
+++ b/solution.py
@@ -1,9 +1,15 @@
+import functools
+
 import jax
 import jax.numpy as jnp
 from jax import lax
+from jax.experimental import pallas as pl
+from jax.experimental.pallas import tpu as pltpu
 from jax.sharding import PartitionSpec as P
 
 ITERS = 2
+TILE = 128
+VMEM_BYTES = 48 * 1024 * 1024
 
 
 def from_partner(value, axis, apart):
@@ -19,10 +25,10 @@
     return lax.psum_scatter(total, "sub", scatter_dimension=1, tiled=True)
 
 
-def body(
+def dense_plan(
     amplitudes, driver, integrals, pair_energy, col_energy, tile_irrep, pair_irrep, mirror_slot
 ):
-    col_irrep = jnp.repeat(tile_irrep, 128)
+    col_irrep = jnp.repeat(tile_irrep, TILE)
     occupied = pair_irrep[:, None] == col_irrep[None, :]
     energy_gap = col_energy[None, :] - pair_energy[:, None]
     driver_wide = driver.astype(jnp.float32)
@@ -38,6 +44,308 @@
         )
         current = updated.astype(jnp.bfloat16)
     return updated
+
+
+class Plan:
+    def __init__(self, tiles, slab_tiles, places):
+        self.tiles = tiles
+        self.half = tiles // 2
+        self.slab = slab_tiles
+        self.places = places
+        self.cap = 8 * slab_tiles
+        self.shared = self.cap * 7 // 16
+        self.direct = self.cap - 2 * self.shared
+
+
+def tile_at(index):
+    return pl.ds(pl.multiple_of(index * TILE, TILE), TILE)
+
+
+def all_labels(plan, own, other, sub, labels):
+    for i in range(plan.half):
+        labels[sub * plan.half + i] = own[i]
+        labels[(1 - sub) * plan.half + i] = other[i]
+
+
+def list_tiles(plan, labels, slab, spots):
+    for n in range(plan.cap):
+        spots[n] = 0
+    count = jnp.int32(0)
+    for j in range(plan.slab):
+        here = labels[slab * plan.slab + j]
+        for k in range(plan.tiles):
+            spots[count] = j * plan.tiles + k
+            count += (labels[k] == here).astype(jnp.int32)
+    for n in range(plan.cap):
+        spots[n] = jnp.where(n < count, spots[n], 0)
+
+
+def pack_kernel(
+    plan, own, other, place, mine_ref, their_ref, shared_ref, direct_ref, full_ref, labels, spots,
+    sizes,
+):
+    slab, side, sub = place[0], place[1], place[2]
+    all_labels(plan, own, other, sub, labels)
+    list_tiles(plan, labels, slab, spots)
+
+    def copy(to_ref, first, count):
+        def step(n, _):
+            spot = spots[first + n]
+            j, k = spot // plan.tiles, lax.rem(spot, plan.tiles)
+            rows, cols = tile_at(lax.rem(k, plan.half)), tile_at(j)
+            to_ref[tile_at(n), :] = jnp.where(
+                k // plan.half == sub, mine_ref[rows, cols], their_ref[rows, cols]
+            )
+            return 0
+
+        lax.fori_loop(0, count, step, 0)
+
+    copy(shared_ref, side * plan.shared, plan.shared)
+    copy(direct_ref, 2 * plan.shared, plan.direct)
+
+    for k in range(plan.tiles):
+        sizes[k] = 0
+    for k in range(plan.tiles):
+        sizes[labels[k]] += 1
+    most = jnp.int32(0)
+    for i in range(plan.places):
+        needed = jnp.int32(0)
+        for j in range(plan.slab):
+            needed += sizes[labels[i * plan.slab + j]]
+        most = jnp.maximum(most, needed)
+    full_ref[0] = (most > plan.cap).astype(jnp.int32)
+
+
+def column(row):
+    n = row.shape[1]
+    here = lax.broadcasted_iota(jnp.int32, (n, n), 0) == lax.broadcasted_iota(jnp.int32, (n, n), 1)
+    return jnp.sum(jnp.where(here, row.astype(jnp.float32), 0.0), axis=1, keepdims=True)
+
+
+def mirror_table(slot_row):
+    n = slot_row.shape[1]
+    slots = column(slot_row).astype(jnp.int32)
+    return lax.broadcasted_iota(jnp.int32, (n, n), 1) == slots
+
+
+def mirror_kernel(plan, own, amps_ref, other_amps_ref, label_row, slot_row, after_ref, cur_ref):
+    rows = amps_ref.shape[0]
+    table = mirror_table(slot_row[...]).astype(jnp.bfloat16)
+    row_label = column(label_row[...]).astype(jnp.int32)
+    zero = jnp.zeros((), cur_ref.dtype)
+    for j in range(plan.half):
+        cols = slice(j * TILE, (j + 1) * TILE)
+        occupied = row_label == own[j]
+        cur_ref[:rows, cols] = jnp.where(occupied, amps_ref[:, cols], zero)
+        mirrored = jnp.dot(table, other_amps_ref[:, cols], preferred_element_type=jnp.float32)
+        cur_ref[rows:, cols] = jnp.where(occupied, mirrored, 0.0).astype(cur_ref.dtype)
+
+
+def multiply(plan, own, place, cur_mine, cur_their, ints_ref, row_label, energies, drivers,
+             col_energy, out_ref):
+    sub = place[2]
+    rows_half = plan.half * TILE
+    mine_at = pl.ds(pl.multiple_of(sub * rows_half, TILE), rows_half)
+    their_at = pl.ds(pl.multiple_of((1 - sub) * rows_half, TILE), rows_half)
+    rows = row_label.shape[0]
+    wide = 2 * TILE
+
+    def block(c, _):
+        cols = pl.ds(pl.multiple_of(c * wide, wide), wide)
+        total = jnp.dot(
+            cur_mine[...], ints_ref[mine_at, cols], preferred_element_type=jnp.float32
+        ) + jnp.dot(cur_their[...], ints_ref[their_at, cols], preferred_element_type=jnp.float32)
+        sym = total[:rows] + total[rows:]
+        for t in range(2):
+            at = pl.ds(pl.multiple_of(c * wide + t * TILE, TILE), TILE)
+            part = sym[:, t * TILE : (t + 1) * TILE]
+            occupied = row_label == own[2 * c + t]
+            energy = col_energy[:, at]
+            for i, (pair_energy, driver) in enumerate(zip(energies, drivers)):
+                new = (driver[:, at].astype(jnp.float32) + part) / (energy - pair_energy)
+                new = jnp.where(occupied, new, 0.0)
+                out_ref[i * rows : (i + 1) * rows, at] = new.astype(out_ref.dtype)
+        return 0
+
+    lax.fori_loop(0, plan.half // 2, block, 0)
+
+
+def first_kernel(plan, rounds, *refs):
+    own, other, place, mine_ref, their_ref = refs[:5]
+    parts = refs[5 : 5 + 3 * rounds]
+    (cur_mine, cur_their, driver, other_driver, label_row, slot_row, energy_row, other_energy_row,
+     col_energy) = refs[5 + 3 * rounds : 14 + 3 * rounds]
+    ints_ref, cur_ref, mirror_driver, labels, spots = refs[14 + 3 * rounds :]
+    z, side, sub = place[0], place[1], place[2]
+    half_places = plan.places // 2
+    width = plan.slab * TILE
+    rows_half = plan.half * TILE
+    ints_ref[...] = jnp.zeros_like(ints_ref)
+    all_labels(plan, own, other, sub, labels)
+
+    def fill(slab, rs, xs, us):
+        first = (slab - sub * half_places) * plan.slab
+        list_tiles(plan, labels, slab, spots)
+
+        def put(n, value):
+            spot = spots[n]
+            j, k = spot // plan.tiles, lax.rem(spot, plan.tiles)
+            ints_ref[tile_at(k), tile_at(first + j)] = value
+
+        def step(n, _):
+            a, b = rs[tile_at(n), :], xs[tile_at(n), :]
+            put(n, jnp.where(side == 0, a, b))
+            put(plan.shared + n, jnp.where(side == 0, b, a))
+            return 0
+
+        lax.fori_loop(0, plan.shared, step, 0)
+
+        def step_direct(n, _):
+            put(2 * plan.shared + n, us[tile_at(n), :])
+            return 0
+
+        lax.fori_loop(0, plan.direct, step_direct, 0)
+
+    for r in range(1, rounds):
+        slab = lax.rem(z - r + plan.places, plan.places)
+        slab = jnp.where(
+            slab // half_places == sub, slab, lax.rem(slab + half_places, plan.places)
+        )
+        fill(slab, *parts[3 * r : 3 * r + 3])
+
+    @pl.when(z // half_places == sub)
+    def _():
+        cols = pl.ds(pl.multiple_of((z - sub * half_places) * width, TILE), width)
+        mine_at = pl.ds(pl.multiple_of(sub * rows_half, TILE), rows_half)
+        their_at = pl.ds(pl.multiple_of((1 - sub) * rows_half, TILE), rows_half)
+        ints_ref[mine_at, cols] = mine_ref[...]
+        ints_ref[their_at, cols] = their_ref[...]
+
+    @pl.when(z // half_places != sub)
+    def _():
+        fill(lax.rem(z + half_places, plan.places), *parts[:3])
+
+    table = mirror_table(slot_row[...])
+    mirror_driver[...] = jnp.dot(
+        table.astype(jnp.bfloat16), other_driver[...], preferred_element_type=jnp.float32
+    ).astype(mirror_driver.dtype)
+    mirror_energy = jnp.sum(jnp.where(table, other_energy_row[...], 0.0), axis=1, keepdims=True)
+    multiply(
+        plan, own, place, cur_mine, cur_their, ints_ref, column(label_row[...]).astype(jnp.int32),
+        (column(energy_row[...]), mirror_energy), (driver, mirror_driver), col_energy, cur_ref,
+    )
+
+
+def second_kernel(plan, own, place, cur_mine, cur_their, ints_ref, driver, label_row, energy_row,
+                  col_energy, out_ref):
+    multiply(
+        plan, own, place, cur_mine, cur_their, ints_ref, column(label_row[...]).astype(jnp.int32),
+        (column(energy_row[...]),), (driver,), col_energy, out_ref,
+    )
+
+
+def call(kernel, smem, vmem, outs, scratch=(), anywhere=(), flag=False, flops=0):
+    moved = sum(v.size * v.dtype.itemsize for v in vmem)
+    in_smem, in_vmem = pl.BlockSpec(memory_space=pltpu.SMEM), pl.BlockSpec(memory_space=pltpu.VMEM)
+    in_any = pl.BlockSpec(memory_space=pl.ANY)
+    return pl.pallas_call(
+        kernel,
+        out_shape=list(outs) + [jax.ShapeDtypeStruct((1,), jnp.int32)] * flag,
+        in_specs=[in_smem] * len(smem) + [in_vmem] * len(vmem) + [in_any] * len(anywhere),
+        out_specs=[in_vmem] * len(outs) + [in_smem] * flag,
+        scratch_shapes=scratch,
+        compiler_params=pltpu.CompilerParams(vmem_limit_bytes=VMEM_BYTES),
+        cost_estimate=pl.CostEstimate(flops=flops, bytes_accessed=2 * moved, transcendentals=0),
+    )(*smem, *vmem, *anywhere)
+
+
+def body(
+    amplitudes, driver, integrals, pair_energy, col_energy, tile_irrep, pair_irrep, mirror_slot
+):
+    places, sides = lax.axis_size("virt"), lax.axis_size("pair")
+    partner_bit = sides.bit_length() - 2
+    rows, half_cols = amplitudes.shape
+    plan = Plan(2 * half_cols // TILE, integrals.shape[1] // TILE, places)
+    half_places = places // 2
+    z, sub = lax.axis_index("virt"), lax.axis_index("sub")
+    side = (lax.axis_index("pair") >> partner_bit) & 1
+    place = jnp.stack([z, side, sub]).astype(jnp.int32)
+
+    def like(shape, dtype=integrals.dtype):
+        return jax.ShapeDtypeStruct(shape, dtype)
+
+    other_irrep = from_partner(tile_irrep, "sub", 0)
+    their_ints = from_partner(integrals, "sub", 0)
+    other_amps = from_partner(amplitudes, "pair", partner_bit)
+    other_driver = from_partner(driver, "pair", partner_bit)
+    other_energy = from_partner(pair_energy, "pair", partner_bit)
+
+    lists = [pltpu.SMEM((plan.tiles,), jnp.int32), pltpu.SMEM((plan.slab * plan.tiles + 1,), jnp.int32)]
+    shared, direct, full = call(
+        functools.partial(pack_kernel, plan),
+        (tile_irrep, other_irrep, place),
+        (integrals, their_ints),
+        [like((plan.shared * TILE, TILE)), like((plan.direct * TILE, TILE))],
+        lists + [pltpu.SMEM((plan.tiles,), jnp.int32)],
+        flag=True,
+    )
+    groups = lax.axis_size("groups")
+    ends = full
+    for apart in range(1, groups):
+        ends = jnp.maximum(
+            ends, lax.ppermute(full, "groups", [(i, (i + apart) % groups) for i in range(groups)])
+        )
+    parts = []
+    for r in range(half_places):
+        pairs = []
+        for i in range(places):
+            for core in range(2):
+                to = (i + r + half_places * (1 - core)) % places
+                if to != i:
+                    pairs.append((2 * i + core, 2 * to + i // half_places))
+        got_shared = lax.ppermute(shared, ("virt", "sub"), pairs)
+        got_direct = lax.ppermute(direct, ("virt", "sub"), pairs)
+        parts += [got_shared, from_partner(got_shared, "pair", partner_bit), got_direct]
+
+    label_row, slot_row = pair_irrep[None, :], mirror_slot[None, :]
+    (cur_mine,) = call(
+        functools.partial(mirror_kernel, plan),
+        (tile_irrep,),
+        (amplitudes, other_amps, label_row, slot_row),
+        [like((2 * rows, half_cols))],
+        anywhere=(direct,),
+    )
+    cur_their = from_partner(cur_mine, "sub", 0)
+
+    energy_row, energy = pair_energy[None, :], col_energy[None, :]
+    flops = 2 * 2 * rows * plan.tiles * TILE * half_cols
+    ints, cur_mine = call(
+        functools.partial(first_kernel, plan, half_places),
+        (tile_irrep, other_irrep, place),
+        (integrals, their_ints, *parts, cur_mine, cur_their, driver, other_driver, label_row,
+         slot_row, energy_row, other_energy[None, :], energy),
+        [like((plan.tiles * TILE, half_cols)), like((2 * rows, half_cols))],
+        [pltpu.VMEM((rows, half_cols), driver.dtype)] + lists,
+        flops=flops,
+    )
+    cur_their = from_partner(cur_mine, "sub", 0)
+
+    def sparse_end():
+        return call(
+            functools.partial(second_kernel, plan),
+            (tile_irrep, place),
+            (cur_mine, cur_their, ints, driver, label_row, energy_row, energy),
+            [like((rows, half_cols), jnp.float32)],
+            flops=flops,
+        )[0]
+
+    def dense_end():
+        return dense_plan(
+            amplitudes, driver, integrals, pair_energy, col_energy, tile_irrep, pair_irrep,
+            mirror_slot,
+        )
+
+    return lax.cond(ends[0] > 0, dense_end, sparse_end)
 
 
 def solution(mesh):

time: 180 us -> 91.1 us (0.51)
  waiting for transfers between devices: 150 us -> 38.5 us
  starting transfers between devices: 3.53 us -> 24.1 us
  Pallas kernels: 0 us -> 12.5 us
  matrix products: 9.83 us -> 0 us
    all_gather x1 -> x0, waiting for transfers between devices: 85 us -> none  [contract(): lax.all_gather(integrals, 'virt', axis=1, tiled=True)]
    ppermute x2 -> x9, waiting for transfers between devices: 44.9 us -> 25.5 us  [from_partner(): lax.ppermute(value, axis, [(i, i ^ 1 << apart) for i in range(lax.axis_si...]
    reduce_scatter x2 -> x0, waiting for transfers between devices: 18.9 us -> none  [contract(): return lax.psum_scatter(total, 'sub', scatter_dimension=1, tiled=True)]
    ppermute x0 -> x5, waiting for transfers between devices: none -> 13 us  [the longest x2 8.23 us: body(): got_shared = lax.ppermute(shared, ('virt', 'sub'), pairs)]
    ppermute x0 -> x5, starting transfers between devices: none -> 12.6 us  [the longest x2 5.77 us: body(): got_direct = lax.ppermute(direct, ('virt', 'sub'), pairs)]
    pallas_call x0 -> x4, Pallas kernels: none -> 12.5 us  [call(): pl.pallas_call(kernel, out_shape=list(outs) + [jax.ShapeDtypeStruct((1,),...]
    dot_general x2 -> x0, matrix products: 9.83 us -> none  [contract(): jnp.dot(blocks[0], lax.all_gather(integrals, 'virt', axis=1, tiled=True),...]
    ppermute x2 -> x9, starting transfers between devices: 3.44 us -> 11.4 us  [from_partner(): lax.ppermute(value, axis, [(i, i ^ 1 << apart) for i in range(lax.axis_si...]
  transfers between devices with their start and end apart: 5 -> 14, of which waited for: 5 -> 8; matrix products, arithmetic and copies ran while one was open for 0% -> 0% of each run, Pallas kernels for 0% -> 3%
where the time goes in v2:
time: 91.1 us; the launch traced here: 90.9 us
  waiting for transfers between devices  38.5 us (42%)
  starting transfers between devices  24.1 us (26%)
  between operations  14.8 us (16%)
  Pallas kernels  12.5 us (14%)
  local copies, waits for them, and re-layouts  0.97 us (1%)
    ppermute x9, waiting for transfers between devices, from_partner(): lax.ppermute(value, axis, [(i, i ^ 1 << apart) for i in range(lax.axis_si...  25.5 us
    pallas_call x4, Pallas kernels, call(): pl.pallas_call(kernel, out_shape=list(outs) + [jax.ShapeDtypeStruct((1,),...  12.5 us
    ppermute x9, starting transfers between devices, from_partner(): lax.ppermute(value, axis, [(i, i ^ 1 << apart) for i in range(lax.axis_si...  11.4 us
    ppermute x2, waiting for transfers between devices, body(): got_shared = lax.ppermute(shared, ('virt', 'sub'), pairs)  8.23 us
    ppermute x2, starting transfers between devices, body(): got_direct = lax.ppermute(direct, ('virt', 'sub'), pairs)  5.77 us
    ppermute x2, starting transfers between devices, body(): got_shared = lax.ppermute(shared, ('virt', 'sub'), pairs)  5.33 us
    ppermute x2, waiting for transfers between devices, body(): got_direct = lax.ppermute(direct, ('virt', 'sub'), pairs)  2.62 us
    ppermute x1, waiting for transfers between devices, body(): lax.ppermute(full, 'groups', [(i, (i + apart) % groups) for i in range(gr...  2.11 us
  transfers between devices with their start and end apart: 14, of which 8 were waited for; matrix products, arithmetic and copies ran while one was open for 0% of the time, Pallas kernels for 3%

profile of v2, /device:TPU:0, one launch (start us, length us, event | category | flops | bytes accessed | tf_op | source)
XLA Modules:
  0.0 90.9 jit_solution(14697476044710878615)
XLA Ops:
  6.6 0.5 collective-permute-start.3
  7.1 2.6 %collective-permute-start.11 = (bf16[240,1024]{1,0:T(8,128)(2,1)}, bf16[240,1024]{1,0:T(8,128)(2,1)S(1)}, u32[]{:S(2)}, u32[]{:S(2)}) collective-permute-start(bf16[240,1024]{1,0:T(8,128)(2,1)} %amps_ref.1), channel_id=1, source_target_pairs={{0,2},{2,0},{1,3},{3,1},{4,6},{6,4},{5,7},{7,5},{8,10},{10,8},{9,1... | collective-permute-start | bytes 1474568 | tf_op jit(solution)/shard_map/ppermute | solution.py:16
  9.7 0.2 collective-permute-start.2
  9.8 0.1 pad_add_fusion.place.refs_2_
  9.9 1.0 %collective-permute-done.2.other.refs_1_ = s32[8]{0:T(128)S(1)} collective-permute-done((s32[8]{0:T(128)}, s32[8]{0:T(128)S(1)}, u32[]{:S(2)}, u32[]{:S(2)}) %collective-permute-start.2) | collective-permute-done | bytes 64 | tf_op jit(solution)/shard_map/ppermute | solution.py:16
  10.9 0.0 collective-permute-done.3.their_ref.refs_4_
  10.9 2.5 %shard_map.84 = (bf16[1792,128]{1,0:T(8,128)(2,1)S(1)}, bf16[512,128]{1,0:T(8,128)(2,1)S(1)}, s32[1]{0:T(128)}) custom-call(s32[8]{0:T(128)} %refs_0_.1, s32[8]{0:T(128)S(1)} %collective-permute-done.2.other.refs_1_, s32[3]{0:T(128)S(1)} %pad_add_fusion.place.refs_2_, bf16[1024,512]{1,0:T(8,128)(2,1)} %refs_3_.1, ...), custom_call_target="tpu_custom_call" | custom-call | bytes 4194304 | tf_op jit(solution)/shard_map/pallas_call | solution.py:251
  13.4 8.3 %collective-permute-done.11.other_amps_ref = bf16[240,1024]{1,0:T(8,128)(2,1)S(1)} collective-permute-done((bf16[240,1024]{1,0:T(8,128)(2,1)}, bf16[240,1024]{1,0:T(8,128)(2,1)S(1)}, u32[]{:S(2)}, u32[]{:S(2)}) %collective-permute-start.11) | collective-permute-done | bytes 491552 | tf_op jit(solution)/shard_map/ppermute | solution.py:16
  21.7 1.6 %shard_map.85.refs_11_ = bf16[480,1024]{1,0:T(8,128)(2,1)S(1)} custom-call(s32[8]{0:T(128)} %refs_0_.1, bf16[240,1024]{1,0:T(8,128)(2,1)} %amps_ref.1, bf16[240,1024]{1,0:T(8,128)(2,1)S(1)} %collective-permute-done.11.other_amps_ref, s32[1,240]{1,0:T(1,128)} %bitcast.14, s32[1,240]{1,0:T(1,128)} %bitcast.21, bf16[512,128]{1,0:T(8,128)(2,1)S(1)} %get-tuple-element.67.after_ref), custom_call_target="tpu_custom_call" | custom-call | bytes 1969920 | tf_op jit(solution)/shard_map/pallas_call | solution.py:251
  23.2 0.0 copy-start.3
  23.3 0.1 collective-permute-start.12
  23.3 3.9 %collective-permute-start.8 = (bf16[1792,128]{1,0:T(8,128)(2,1)S(1)}, bf16[1792,128]{1,0:T(8,128)(2,1)S(1)}, u32[]{:S(2)}, u32[]{:S(2)}) collective-permute-start(bf16[1792,128]{1,0:T(8,128)(2,1)S(1)} %get-tuple-element.66), channel_id=1, source_target_pairs={{0,12},{1,4},{4,0},{5,8},{8,5},{9,13},{12,9},{13,1},{2,14},{3,6},{... | collective-permute-start | bytes 1376264 | tf_op jit(solution)/shard_map/ppermute | solution.py:306
  27.3 1.4 %collective-permute-start.5 = (bf16[1792,128]{1,0:T(8,128)(2,1)S(1)}, bf16[1792,128]{1,0:T(8,128)(2,1)S(1)}, u32[]{:S(2)}, u32[]{:S(2)}) collective-permute-start(bf16[1792,128]{1,0:T(8,128)(2,1)S(1)} %get-tuple-element.66), channel_id=1, source_target_pairs={{0,8},{4,12},{8,1},{12,5},{2,10},{6,14},{10,3},{14,7},{16,24},{20,... | collective-permute-start | bytes 1376264 | tf_op jit(solution)/shard_map/ppermute | solution.py:306
  28.7 1.6 %collective-permute-start.13 = (bf16[240,1024]{1,0:T(8,128)(2,1)S(1)}, bf16[240,1024]{1,0:T(8,128)(2,1)S(1)}, u32[]{:S(2)}, u32[]{:S(2)}) collective-permute-start(bf16[240,1024]{1,0:T(8,128)(2,1)S(1)} %copy-done.2), channel_id=1, source_target_pairs={{0,2},{2,0},{1,3},{3,1},{4,6},{6,4},{5,7},{7,5},{8,10},{10,8},{9,1... | collective-permute-start | bytes 1474568 | tf_op jit(solution)/shard_map/ppermute | solution.py:16
  30.2 5.6 %collective-permute-done.8.refs_8_ = bf16[1792,128]{1,0:T(8,128)(2,1)S(1)} collective-permute-done((bf16[1792,128]{1,0:T(8,128)(2,1)S(1)}, bf16[1792,128]{1,0:T(8,128)(2,1)S(1)}, u32[]{:S(2)}, u32[]{:S(2)}) %collective-permute-start.8) | collective-permute-done | bytes 458784 | tf_op jit(solution)/shard_map/ppermute | solution.py:306
  35.9 2.1 %collective-permute-start.9 = (bf16[1792,128]{1,0:T(8,128)(2,1)S(1)}, bf16[1792,128]{1,0:T(8,128)(2,1)S(1)}, u32[]{:S(2)}, u32[]{:S(2)}) collective-permute-start(bf16[1792,128]{1,0:T(8,128)(2,1)S(1)} %collective-permute-done.8.refs_8_), channel_id=1, source_target_pairs={{0,2},{2,0},{1,3},{3,1},{4,6},{6,4},{5,7},{7,5},{8,10},{10,8},{9,1... | collective-permute-start | bytes 1376264 | tf_op jit(solution)/shard_map/ppermute | solution.py:16
  37.9 2.6 %collective-permute-done.5.refs_5_ = bf16[1792,128]{1,0:T(8,128)(2,1)S(1)} collective-permute-done((bf16[1792,128]{1,0:T(8,128)(2,1)S(1)}, bf16[1792,128]{1,0:T(8,128)(2,1)S(1)}, u32[]{:S(2)}, u32[]{:S(2)}) %collective-permute-start.5) | collective-permute-done | bytes 458784 | tf_op jit(solution)/shard_map/ppermute | solution.py:306
  40.5 1.5 %collective-permute-start.6 = (bf16[1792,128]{1,0:T(8,128)(2,1)S(1)}, bf16[1792,128]{1,0:T(8,128)(2,1)S(1)}, u32[]{:S(2)}, u32[]{:S(2)}) collective-permute-start(bf16[1792,128]{1,0:T(8,128)(2,1)S(1)} %collective-permute-done.5.refs_5_), channel_id=1, source_target_pairs={{0,2},{2,0},{1,3},{3,1},{4,6},{6,4},{5,7},{7,5},{8,10},{10,8},{9,1... | collective-permute-start | bytes 1376264 | tf_op jit(solution)/shard_map/ppermute | solution.py:16
  42.0 0.5 collective-permute-start.14
  42.6 16.2 %collective-permute-done.14 = f32[240]{0:T(256)S(1)} collective-permute-done((f32[240]{0:T(256)S(1)}, f32[240]{0:T(256)S(1)}, u32[]{:S(2)}, u32[]{:S(2)}) %collective-permute-start.14) | collective-permute-done | bytes 992 | tf_op jit(solution)/shard_map/ppermute | solution.py:16
  58.8 4.5 %collective-permute-start.10 = (bf16[512,128]{1,0:T(8,128)(2,1)S(1)}, bf16[512,128]{1,0:T(8,128)(2,1)S(1)}, u32[]{:S(2)}, u32[]{:S(2)}) collective-permute-start(bf16[512,128]{1,0:T(8,128)(2,1)S(1)} %get-tuple-element.67.after_ref), channel_id=1, source_target_pairs={{0,12},{1,4},{4,0},{5,8},{8,5},{9,13},{12,9},{13,1},{2,14},{3,6},{... | collective-permute-start | bytes 393224 | tf_op jit(solution)/shard_map/ppermute | solution.py:307
  63.3 1.3 %collective-permute-start.7 = (bf16[512,128]{1,0:T(8,128)(2,1)S(1)}, bf16[512,128]{1,0:T(8,128)(2,1)S(1)}, u32[]{:S(2)}, u32[]{:S(2)}) collective-permute-start(bf16[512,128]{1,0:T(8,128)(2,1)S(1)} %get-tuple-element.67.after_ref), channel_id=1, source_target_pairs={{0,8},{4,12},{8,1},{12,5},{2,10},{6,14},{10,3},{14,7},{16,24},{20,... | collective-permute-start | bytes 393224 | tf_op jit(solution)/shard_map/ppermute | solution.py:307
  64.6 1.2 %collective-permute-done.10.refs_10_ = bf16[512,128]{1,0:T(8,128)(2,1)S(1)} collective-permute-done((bf16[512,128]{1,0:T(8,128)(2,1)S(1)}, bf16[512,128]{1,0:T(8,128)(2,1)S(1)}, u32[]{:S(2)}, u32[]{:S(2)}) %collective-permute-start.10) | collective-permute-done | bytes 131104 | tf_op jit(solution)/shard_map/ppermute | solution.py:307
  65.8 1.4 %collective-permute-done.7.refs_7_ = bf16[512,128]{1,0:T(8,128)(2,1)S(1)} collective-permute-done((bf16[512,128]{1,0:T(8,128)(2,1)S(1)}, bf16[512,128]{1,0:T(8,128)(2,1)S(1)}, u32[]{:S(2)}, u32[]{:S(2)}) %collective-permute-start.7) | collective-permute-done | bytes 131104 | tf_op jit(solution)/shard_map/ppermute | solution.py:307
  67.3 4.9 %shard_map.86 = (bf16[2048,1024]{1,0:T(8,128)(2,1)S(1)}, bf16[480,1024]{1,0:T(8,128)(2,1)S(1)}) custom-call(s32[8]{0:T(128)S(1)} %copy-done.7, s32[8]{0:T(128)S(1)} %collective-permute-done.2.other.refs_1_, s32[3]{0:T(128)S(1)} %pad_add_fusion.place.refs_2_, bf16[1024,512]{1,0:T(8,128)(2,1)S(1)} %copy-done, ...), custom_call_target="tpu_custom_call" | custom-call | flops 2013265920 | bytes 14302720 | tf_op jit(solution)/shard_map/pallas_call | solution.py:251
  72.2 2.5 %collective-permute-start.15 = (bf16[480,1024]{1,0:T(8,128)(2,1)S(1)}, bf16[480,1024]{1,0:T(8,128)(2,1)S(1)}, u32[]{:S(2)}, u32[]{:S(2)}) collective-permute-start(bf16[480,1024]{1,0:T(8,128)(2,1)S(1)} %get-tuple-element.68), channel_id=1, source_target_pairs={{0,1},{1,0},{2,3},{3,2},{4,5},{5,4},{6,7},{7,6},{8,9},{9,8},{10,11... | collective-permute-start | bytes 2949128 | tf_op jit(solution)/shard_map/ppermute | solution.py:16
  74.6 1.5 %collective-permute-start.4 = (s32[1]{0:T(128)}, s32[1]{0:T(128)}, u32[]{:S(2)}, u32[]{:S(2)}) collective-permute-start(s32[1]{0:T(128)} %get-tuple-element.65), channel_id=1, source_target_pairs={{0,16},{16,0},{1,17},{17,1},{2,18},{18,2},{3,19},{19,3},{4,20},{20... | collective-permute-start | bytes 20 | tf_op jit(solution)/shard_map/ppermute | solution.py:296
  76.2 2.1 %collective-permute-done.4 = s32[1]{0:T(128)} collective-permute-done((s32[1]{0:T(128)}, s32[1]{0:T(128)}, u32[]{:S(2)}, u32[]{:S(2)}) %collective-permute-start.4) | collective-permute-done | bytes 36 | tf_op jit(solution)/shard_map/ppermute | solution.py:296
  79.6 3.6 %conditional.1 = (f32[240,1024]{1,0:T(8,128)S(1)}) conditional(s32[]{:T(128)} %bitcast.4, (s32[8]{0:T(128)S(1)}, s32[3]{0:T(128)S(1)}, bf16[480,1024]{1,0:T(8,128)(2,1)S(1)}, bf16[480,1024]{1,0:T(8,128)(2,1)S(1)}, bf16[2048,1024]{1,0:T(8,128)(2,1)S(1)}, /*index=5*/bf16[240,1024]{1,0:T(8,128)(2,1)S(1)}, s32[1,240]{1,0:T(1,128)S(1)}, ...), branch_computations={%region_0.0_spmd, %region_1.5_spmd} | conditional | flops 2017938560 | bytes 68164888 | solution.py:348
  79.6 3.5 %branch_0_fun.1 = f32[240,1024]{1,0:T(8,128)S(1)} custom-call(s32[8]{0:T(128)S(1)} %get-tuple-element.42.own, s32[3]{0:T(128)S(1)} %get-tuple-element.44.place, bf16[480,1024]{1,0:T(8,128)(2,1)S(1)} %get-tuple-element.45.cur_mine, bf16[480,1024]{1,0:T(8,128)(2,1)S(1)} %get-tuple-element.46.cur_their, bf16[2048,1024]{1,0:T(8,128)(2,1)S(1)} %get-tuple-element.47.ints_ref, ...), custom_call_target="tpu_custom_call" | custom-call | flops 2013265920 | bytes 13315840 | tf_op jit(solution)/shard_map/cond/branch_0_fun/pallas_call | solution.py:251
  83.1 0.0 copy-start.4
  83.1 0.9 %copy-done.4 = f32[240,1024]{1,0:T(8,128)} copy-done((f32[240,1024]{1,0:T(8,128)}, f32[240,1024]{1,0:T(8,128)S(1)}, u32[]{:S(2)}) %copy-start.4) | copy-done | bytes 983064
  (20 shorter events, 0.0 us)
Async XLA Ops:
  6.5 60.7 %copy-start = (bf16[1024,512]{1,0:T(8,128)(2,1)S(1)}, bf16[1024,512]{1,0:T(8,128)(2,1)}, u32[]{:S(2)}) copy-start(bf16[1024,512]{1,0:T(8,128)(2,1)} %refs_3_.1) | copy-start | bytes 3145732
  6.5 60.7 %copy-start.7 = (s32[8]{0:T(128)S(1)}, s32[8]{0:T(128)}, u32[]{:S(2)}) copy-start(s32[8]{0:T(128)} %refs_0_.1) | copy-start | bytes 100
  6.5 60.7 %copy-start.9 = (s32[240]{0:T(256)S(1)}, s32[240]{0:T(256)}, u32[]{:S(2)}) copy-start(s32[240]{0:T(256)} %param.19) | copy-start | bytes 2884
  6.5 60.7 %copy-start.5 = (s32[240]{0:T(256)S(1)}, s32[240]{0:T(256)}, u32[]{:S(2)}) copy-start(s32[240]{0:T(256)} %param.18) | copy-start | bytes 2884
  6.5 22.1 %copy-start.2 = (bf16[240,1024]{1,0:T(8,128)(2,1)S(1)}, bf16[240,1024]{1,0:T(8,128)(2,1)}, u32[]{:S(2)}) copy-start(bf16[240,1024]{1,0:T(8,128)(2,1)} %refs_13_.1) | copy-start | bytes 1474564
  6.5 35.5 %copy-start.8 = (f32[240]{0:T(256)S(1)}, f32[240]{0:T(256)}, u32[]{:S(2)}) copy-start(f32[240]{0:T(256)} %param.15) | copy-start | bytes 2884
  6.6 60.7 %copy-start.6 = (f32[1024]{0:T(1024)S(1)}, f32[1024]{0:T(1024)}, u32[]{:S(2)}) copy-start(f32[1024]{0:T(1024)} %param.16) | copy-start | bytes 12292
  6.6 4.3 %collective-permute-start.3 = (bf16[1024,512]{1,0:T(8,128)(2,1)}, bf16[1024,512]{1,0:T(8,128)(2,1)S(1)}, u32[]{:S(2)}, u32[]{:S(2)}) collective-permute-start(bf16[1024,512]{1,0:T(8,128)(2,1)} %refs_3_.1), channel_id=1, source_target_pairs={{0,1},{1,0},{2,3},{3,2},{4,5},{5,4},{6,7},{7,6},{8,9},{9,8},{10,11... | collective-permute-start | bytes 3145736 | tf_op jit(solution)/shard_map/ppermute | solution.py:16
  7.1 14.6 %collective-permute-start.11 = (bf16[240,1024]{1,0:T(8,128)(2,1)}, bf16[240,1024]{1,0:T(8,128)(2,1)S(1)}, u32[]{:S(2)}, u32[]{:S(2)}) collective-permute-start(bf16[240,1024]{1,0:T(8,128)(2,1)} %amps_ref.1), channel_id=1, source_target_pairs={{0,2},{2,0},{1,3},{3,1},{4,6},{6,4},{5,7},{7,5},{8,10},{10,8},{9,1... | collective-permute-start | bytes 1474568 | tf_op jit(solution)/shard_map/ppermute | solution.py:16
  9.7 1.3 %collective-permute-start.2 = (s32[8]{0:T(128)}, s32[8]{0:T(128)S(1)}, u32[]{:S(2)}, u32[]{:S(2)}) collective-permute-start(s32[8]{0:T(128)} %refs_0_.1), channel_id=1, source_target_pairs={{0,1},{1,0},{2,3},{3,2},{4,5},{5,4},{6,7},{7,6},{8,9},{9,8},{10,11... | collective-permute-start | bytes 104 | tf_op jit(solution)/shard_map/ppermute | solution.py:16
  23.2 56.3 %copy-start.3 = (bf16[240,1024]{1,0:T(8,128)(2,1)S(1)}, bf16[240,1024]{1,0:T(8,128)(2,1)}, u32[]{:S(2)}) copy-start(bf16[240,1024]{1,0:T(8,128)(2,1)} %amps_ref.1) | copy-start | bytes 1474564
  23.3 44.0 %collective-permute-start.12 = (bf16[480,1024]{1,0:T(8,128)(2,1)S(1)}, bf16[480,1024]{1,0:T(8,128)(2,1)S(1)}, u32[]{:S(2)}, u32[]{:S(2)}) collective-permute-start(bf16[480,1024]{1,0:T(8,128)(2,1)S(1)} %shard_map.85.refs_11_), channel_id=1, source_target_pairs={{0,1},{1,0},{2,3},{3,2},{4,5},{5,4},{6,7},{7,6},{8,9},{9,8},{10,11... | collective-permute-start | bytes 2949128 | tf_op jit(solution)/shard_map/ppermute | solution.py:16
  23.3 12.5 %collective-permute-start.8 = (bf16[1792,128]{1,0:T(8,128)(2,1)S(1)}, bf16[1792,128]{1,0:T(8,128)(2,1)S(1)}, u32[]{:S(2)}, u32[]{:S(2)}) collective-permute-start(bf16[1792,128]{1,0:T(8,128)(2,1)S(1)} %get-tuple-element.66), channel_id=1, source_target_pairs={{0,12},{1,4},{4,0},{5,8},{8,5},{9,13},{12,9},{13,1},{2,14},{3,6},{... | collective-permute-start | bytes 1376264 | tf_op jit(solution)/shard_map/ppermute | solution.py:306
  27.3 13.3 %collective-permute-start.5 = (bf16[1792,128]{1,0:T(8,128)(2,1)S(1)}, bf16[1792,128]{1,0:T(8,128)(2,1)S(1)}, u32[]{:S(2)}, u32[]{:S(2)}) collective-permute-start(bf16[1792,128]{1,0:T(8,128)(2,1)S(1)} %get-tuple-element.66), channel_id=1, source_target_pairs={{0,8},{4,12},{8,1},{12,5},{2,10},{6,14},{10,3},{14,7},{16,24},{20,... | collective-permute-start | bytes 1376264 | tf_op jit(solution)/shard_map/ppermute | solution.py:306
  28.7 34.6 %collective-permute-start.13 = (bf16[240,1024]{1,0:T(8,128)(2,1)S(1)}, bf16[240,1024]{1,0:T(8,128)(2,1)S(1)}, u32[]{:S(2)}, u32[]{:S(2)}) collective-permute-start(bf16[240,1024]{1,0:T(8,128)(2,1)S(1)} %copy-done.2), channel_id=1, source_target_pairs={{0,2},{2,0},{1,3},{3,1},{4,6},{6,4},{5,7},{7,5},{8,10},{10,8},{9,1... | collective-permute-start | bytes 1474568 | tf_op jit(solution)/shard_map/ppermute | solution.py:16
  35.9 31.4 %collective-permute-start.9 = (bf16[1792,128]{1,0:T(8,128)(2,1)S(1)}, bf16[1792,128]{1,0:T(8,128)(2,1)S(1)}, u32[]{:S(2)}, u32[]{:S(2)}) collective-permute-start(bf16[1792,128]{1,0:T(8,128)(2,1)S(1)} %collective-permute-done.8.refs_8_), channel_id=1, source_target_pairs={{0,2},{2,0},{1,3},{3,1},{4,6},{6,4},{5,7},{7,5},{8,10},{10,8},{9,1... | collective-permute-start | bytes 1376264 | tf_op jit(solution)/shard_map/ppermute | solution.py:16
  40.5 26.7 %collective-permute-start.6 = (bf16[1792,128]{1,0:T(8,128)(2,1)S(1)}, bf16[1792,128]{1,0:T(8,128)(2,1)S(1)}, u32[]{:S(2)}, u32[]{:S(2)}) collective-permute-start(bf16[1792,128]{1,0:T(8,128)(2,1)S(1)} %collective-permute-done.5.refs_5_), channel_id=1, source_target_pairs={{0,2},{2,0},{1,3},{3,1},{4,6},{6,4},{5,7},{7,5},{8,10},{10,8},{9,1... | collective-permute-start | bytes 1376264 | tf_op jit(solution)/shard_map/ppermute | solution.py:16
  42.0 16.8 %collective-permute-start.14 = (f32[240]{0:T(256)S(1)}, f32[240]{0:T(256)S(1)}, u32[]{:S(2)}, u32[]{:S(2)}) collective-permute-start(f32[240]{0:T(256)S(1)} %copy-done.8), channel_id=1, source_target_pairs={{0,2},{2,0},{1,3},{3,1},{4,6},{6,4},{5,7},{7,5},{8,10},{10,8},{9,1... | collective-permute-start | bytes 2888 | tf_op jit(solution)/shard_map/ppermute | solution.py:16
  58.8 7.0 %collective-permute-start.10 = (bf16[512,128]{1,0:T(8,128)(2,1)S(1)}, bf16[512,128]{1,0:T(8,128)(2,1)S(1)}, u32[]{:S(2)}, u32[]{:S(2)}) collective-permute-start(bf16[512,128]{1,0:T(8,128)(2,1)S(1)} %get-tuple-element.67.after_ref), channel_id=1, source_target_pairs={{0,12},{1,4},{4,0},{5,8},{8,5},{9,13},{12,9},{13,1},{2,14},{3,6},{... | collective-permute-start | bytes 393224 | tf_op jit(solution)/shard_map/ppermute | solution.py:307
  63.3 3.9 %collective-permute-start.7 = (bf16[512,128]{1,0:T(8,128)(2,1)S(1)}, bf16[512,128]{1,0:T(8,128)(2,1)S(1)}, u32[]{:S(2)}, u32[]{:S(2)}) collective-permute-start(bf16[512,128]{1,0:T(8,128)(2,1)S(1)} %get-tuple-element.67.after_ref), channel_id=1, source_target_pairs={{0,8},{4,12},{8,1},{12,5},{2,10},{6,14},{10,3},{14,7},{16,24},{20,... | collective-permute-start | bytes 393224 | tf_op jit(solution)/shard_map/ppermute | solution.py:307
  72.2 7.4 %collective-permute-start.15 = (bf16[480,1024]{1,0:T(8,128)(2,1)S(1)}, bf16[480,1024]{1,0:T(8,128)(2,1)S(1)}, u32[]{:S(2)}, u32[]{:S(2)}) collective-permute-start(bf16[480,1024]{1,0:T(8,128)(2,1)S(1)} %get-tuple-element.68), channel_id=1, source_target_pairs={{0,1},{1,0},{2,3},{3,2},{4,5},{5,4},{6,7},{7,6},{8,9},{9,8},{10,11... | collective-permute-start | bytes 2949128 | tf_op jit(solution)/shard_map/ppermute | solution.py:16
  74.6 3.6 %collective-permute-start.4 = (s32[1]{0:T(128)}, s32[1]{0:T(128)}, u32[]{:S(2)}, u32[]{:S(2)}) collective-permute-start(s32[1]{0:T(128)} %get-tuple-element.65), channel_id=1, source_target_pairs={{0,16},{16,0},{1,17},{17,1},{2,18},{18,2},{3,19},{19,3},{4,20},{20... | collective-permute-start | bytes 20 | tf_op jit(solution)/shard_map/ppermute | solution.py:296
  83.1 0.9 %copy-start.4 = (f32[240,1024]{1,0:T(8,128)}, f32[240,1024]{1,0:T(8,128)S(1)}, u32[]{:S(2)}) copy-start(f32[240,1024]{1,0:T(8,128)S(1)} %get-tuple-element.111) | copy-start | bytes 2949124

commit v3 on v0

--- a/solution.py
+++ b/solution.py
@@ -1,9 +1,15 @@
+import functools
+
 import jax
 import jax.numpy as jnp
 from jax import lax
+from jax.experimental import pallas as pl
+from jax.experimental.pallas import tpu as pltpu
 from jax.sharding import PartitionSpec as P
 
 ITERS = 2
+TILE = 128
+VMEM_BYTES = 48 * 1024 * 1024
 
 
 def from_partner(value, axis, apart):
@@ -11,18 +17,28 @@
 
 
 def contract(blocks, integrals):
-    total = jnp.dot(
-        blocks[0],
-        lax.all_gather(integrals, "virt", axis=1, tiled=True),
-        preferred_element_type=jnp.float32,
-    )
-    return lax.psum_scatter(total, "sub", scatter_dimension=1, tiled=True)
-
-
-def body(
+    places, z, sub = lax.axis_size("virt"), lax.axis_index("virt"), lax.axis_index("sub")
+    width = integrals.shape[1]
+    whole = jnp.zeros((integrals.shape[0], places * width), integrals.dtype)
+    for apart in range(places):
+        slab = integrals
+        if apart:
+            slab = lax.ppermute(
+                integrals, "virt", [(i, (i + apart) % places) for i in range(places)]
+            )
+        at = lax.rem(z - apart + places, places) * width
+        whole = lax.dynamic_update_slice(whole, slab, (0, at))
+    total = jnp.dot(blocks[0], whole, preferred_element_type=jnp.float32)
+    half = total.shape[1] // 2
+    mine = lax.dynamic_slice_in_dim(total, sub * half, half, 1)
+    theirs = lax.dynamic_slice_in_dim(total, (1 - sub) * half, half, 1)
+    return mine + from_partner(theirs, "sub", 0)
+
+
+def dense_plan(
     amplitudes, driver, integrals, pair_energy, col_energy, tile_irrep, pair_irrep, mirror_slot
 ):
-    col_irrep = jnp.repeat(tile_irrep, 128)
+    col_irrep = jnp.repeat(tile_irrep, TILE)
     occupied = pair_irrep[:, None] == col_irrep[None, :]
     energy_gap = col_energy[None, :] - pair_energy[:, None]
     driver_wide = driver.astype(jnp.float32)
@@ -38,6 +54,363 @@
         )
         current = updated.astype(jnp.bfloat16)
     return updated
+
+
+class Plan:
+    def __init__(self, tiles, slab_tiles, places):
+        self.tiles = tiles
+        self.half = tiles // 2
+        self.slab = slab_tiles
+        self.places = places
+        self.near = places // 2
+        self.cap = 8 * slab_tiles
+        self.part = self.cap // 2
+
+
+def tile_at(index):
+    return pl.ds(pl.multiple_of(index * TILE, TILE), TILE)
+
+
+def all_labels(plan, own, other, sub, labels):
+    for i in range(plan.half):
+        labels[sub * plan.half + i] = own[i]
+        labels[(1 - sub) * plan.half + i] = other[i]
+
+
+def list_tiles(plan, labels, slab, spots):
+    for n in range(plan.cap):
+        spots[n] = 0
+    count = jnp.int32(0)
+    for j in range(plan.slab):
+        here = labels[slab * plan.slab + j]
+        for k in range(plan.tiles):
+            spots[count] = j * plan.tiles + k
+            count += (labels[k] == here).astype(jnp.int32)
+    for n in range(plan.cap):
+        spots[n] = jnp.where(n < count, spots[n], 0)
+
+
+def pack_kernel(
+    plan, own, other, place, mine_ref, their_ref, amps_ref, label_row, energy_row, send0_ref,
+    send1_ref, masked_ref, full_ref, labels, spots, sizes,
+):
+    slab, side, sub = place[0], place[1], place[2]
+    all_labels(plan, own, other, sub, labels)
+    list_tiles(plan, labels, slab, spots)
+    is_near = slab // plan.near == sub
+
+    for i, to_ref in enumerate((send0_ref, send1_ref)):
+        first = jnp.where(is_near, i, side) * plan.part
+
+        def step(n, _):
+            spot = spots[first + n]
+            j, k = spot // plan.tiles, lax.rem(spot, plan.tiles)
+            rows, cols = tile_at(lax.rem(k, plan.half)), tile_at(j)
+            to_ref[tile_at(n), :] = jnp.where(
+                k // plan.half == sub, mine_ref[rows, cols], their_ref[rows, cols]
+            )
+            return 0
+
+        lax.fori_loop(0, plan.part, step, 0)
+
+    rows = amps_ref.shape[0]
+    row_label = column(label_row[...]).astype(jnp.int32)
+    for j in range(plan.half):
+        cols = slice(j * TILE, (j + 1) * TILE)
+        amps = amps_ref[:, cols]
+        masked_ref[:rows, cols] = jnp.where(row_label == own[j], amps, jnp.zeros((), amps.dtype))
+
+    masked_ref[rows:, :] = jnp.zeros_like(masked_ref[rows:, :])
+    rest = jnp.broadcast_to(energy_row[...], (16, rows))
+    at = lax.broadcasted_iota(jnp.int32, (16, rows), 0)
+    terms = jnp.zeros((16, rows), jnp.float32)
+    for i in range(3):
+        term = rest.astype(jnp.bfloat16).astype(jnp.float32)
+        terms = jnp.where(at == i, term, terms)
+        rest = rest - term
+    masked_ref[rows:, :rows] = terms.astype(jnp.bfloat16)
+
+    for k in range(plan.tiles):
+        sizes[k] = 0
+    for k in range(plan.tiles):
+        sizes[labels[k]] += 1
+    most = jnp.int32(0)
+    for i in range(plan.places):
+        needed = jnp.int32(0)
+        for j in range(plan.slab):
+            needed += sizes[labels[i * plan.slab + j]]
+        most = jnp.maximum(most, needed)
+    full_ref[0] = (most > plan.cap).astype(jnp.int32)
+
+
+def column(row):
+    n = row.shape[1]
+    here = lax.broadcasted_iota(jnp.int32, (n, n), 0) == lax.broadcasted_iota(jnp.int32, (n, n), 1)
+    return jnp.sum(jnp.where(here, row.astype(jnp.float32), 0.0), axis=1, keepdims=True)
+
+
+def mirror_table(slot_row):
+    n = slot_row.shape[1]
+    slots = column(slot_row).astype(jnp.int32)
+    return lax.broadcasted_iota(jnp.int32, (n, n), 1) == slots
+
+
+def mirror_kernel(
+    masked_ref, other_masked_ref, other_driver_ref, slot_row, label_row, energy_row, after_ref,
+    cur_ref, mirror_driver_ref, columns_ref,
+):
+    rows = mirror_driver_ref.shape[0]
+    table = mirror_table(slot_row[...])
+    weights = table.astype(jnp.bfloat16)
+    cur_ref[:rows, :] = masked_ref[:rows, :]
+    cur_ref[rows:, :] = jnp.dot(
+        weights, other_masked_ref[:rows, :], preferred_element_type=jnp.float32
+    ).astype(cur_ref.dtype)
+    mirror_driver_ref[...] = jnp.dot(
+        weights, other_driver_ref[...], preferred_element_type=jnp.float32
+    ).astype(mirror_driver_ref.dtype)
+    terms = other_masked_ref[rows:, :rows].astype(jnp.float32)
+    other_energy = (terms[0:1] + terms[1:2]) + terms[2:3]
+    mirror_energy = jnp.sum(jnp.where(table, other_energy, 0.0), axis=1, keepdims=True)
+    for i, value in enumerate((column(label_row[...]), column(energy_row[...]), mirror_energy)):
+        columns_ref[i * rows : (i + 1) * rows, :] = jnp.broadcast_to(value, (rows, TILE))
+
+
+def halves(plan, sub):
+    rows = plan.half * TILE
+    return (
+        pl.ds(pl.multiple_of(sub * rows, TILE), rows),
+        pl.ds(pl.multiple_of((1 - sub) * rows, TILE), rows),
+    )
+
+
+WIDE = 2 * TILE
+
+
+def first_kernel(plan, rounds, *refs):
+    own, other, place, ends, mine_ref, their_ref, cur_mine, cur_their, driver, mirror_driver = refs[:10]
+    columns, col_energy = refs[10:12]
+    got = refs[12 : 12 + rounds]
+    swapped = refs[12 + rounds : 12 + rounds + plan.near]
+    ints_ref, cur_ref, end_ref, labels, spots = refs[12 + rounds + plan.near :]
+    z, side, sub = place[0], place[1], place[2]
+    width = plan.slab * TILE
+    mine_at, their_at = halves(plan, sub)
+    end_ref[0] = ends[0]
+    ints_ref[...] = jnp.zeros_like(ints_ref)
+    all_labels(plan, own, other, sub, labels)
+    here = lax.rem(z, plan.near)
+
+    def fill(place, low_ref, high_ref, turn):
+        list_tiles(plan, labels, sub * plan.near + place, spots)
+
+        def put(n, value):
+            spot = spots[n]
+            j, k = spot // plan.tiles, lax.rem(spot, plan.tiles)
+            ints_ref[tile_at(k), tile_at(place * plan.slab + j)] = value
+
+        def step(n, _):
+            low, high = low_ref[tile_at(n), :], high_ref[tile_at(n), :]
+            put(n, jnp.where(turn, high, low))
+            put(plan.part + n, jnp.where(turn, low, high))
+            return 0
+
+        lax.fori_loop(0, plan.part, step, 0)
+
+    @pl.when(z // plan.near == sub)
+    def _():
+        cols = pl.ds(pl.multiple_of(here * width, TILE), width)
+        ints_ref[mine_at, cols] = mine_ref[...]
+        ints_ref[their_at, cols] = their_ref[...]
+        for r in range(1, plan.near):
+            fill(lax.rem(here + plan.near - r, plan.near), got[2 * r - 2], got[2 * r - 1], False)
+
+    @pl.when(z // plan.near != sub)
+    def _():
+        for r in range(plan.near):
+            fill(lax.rem(here + plan.near - r, plan.near), got[r], swapped[r], side == 1)
+
+    rows = driver.shape[0]
+
+    def block(c, _):
+        cols = pl.ds(pl.multiple_of(c * WIDE, WIDE), WIDE)
+        total = jnp.dot(
+            cur_mine[...], ints_ref[mine_at, cols], preferred_element_type=jnp.float32
+        ) + jnp.dot(cur_their[...], ints_ref[their_at, cols], preferred_element_type=jnp.float32)
+        sym = total[:rows] + total[rows:]
+        for t in range(2):
+            at = pl.ds(pl.multiple_of(c * WIDE + t * TILE, TILE), TILE)
+            part = sym[:, t * TILE : (t + 1) * TILE]
+            occupied = columns[:rows] == own[2 * c + t].astype(jnp.float32)
+            for i, source in enumerate((driver, mirror_driver)):
+                gap = col_energy[:, at] - columns[(i + 1) * rows : (i + 2) * rows]
+                new = (source[:, at].astype(jnp.float32) + part) / gap
+                new = jnp.where(occupied, new, 0.0)
+                cur_ref[i * rows : (i + 1) * rows, at] = new.astype(cur_ref.dtype)
+        return 0
+
+    lax.fori_loop(0, plan.half // 2, block, 0)
+
+
+def part_kernel(plan, place, cur_ref, ints_ref, sym_ref):
+    mine_at, _ = halves(plan, place[2])
+    rows = sym_ref.shape[0]
+
+    def block(c, _):
+        cols = pl.ds(pl.multiple_of(c * WIDE, WIDE), WIDE)
+        total = jnp.dot(cur_ref[...], ints_ref[mine_at, cols], preferred_element_type=jnp.float32)
+        sym_ref[:, cols] = total[:rows] + total[rows:]
+        return 0
+
+    lax.fori_loop(0, plan.half // 2, block, 0)
+
+
+def last_kernel(
+    plan, own, place, cur_ref, ints_ref, sym_ref, driver, columns, col_energy, out_ref, new_ref, sems
+):
+    _, their_at = halves(plan, place[2])
+    rows = driver.shape[0]
+    copies = []
+    for c in range(plan.half // 2):
+        cols = slice(c * WIDE, (c + 1) * WIDE)
+        total = jnp.dot(cur_ref[...], ints_ref[their_at, cols], preferred_element_type=jnp.float32)
+        sym = sym_ref[:, cols] + (total[:rows] + total[rows:])
+        for t in range(2):
+            at = slice(c * WIDE + t * TILE, c * WIDE + (t + 1) * TILE)
+            occupied = columns[:rows] == own[2 * c + t].astype(jnp.float32)
+            gap = col_energy[:, at] - columns[rows : 2 * rows]
+            new = (driver[:, at].astype(jnp.float32) + sym[:, t * TILE : (t + 1) * TILE]) / gap
+            new_ref[:, at] = jnp.where(occupied, new, 0.0)
+        copy = pltpu.make_async_copy(new_ref.at[:, cols], out_ref.at[:, cols], sems.at[c])
+        copy.start()
+        copies.append(copy)
+    for copy in copies:
+        copy.wait()
+
+
+def call(kernel, smem, vmem, outs, scratch=(), anywhere=(), flag=False, flops=0, to_any=False):
+    moved = sum(v.size * v.dtype.itemsize for v in vmem)
+    in_smem, in_vmem = pl.BlockSpec(memory_space=pltpu.SMEM), pl.BlockSpec(memory_space=pltpu.VMEM)
+    in_any = pl.BlockSpec(memory_space=pl.ANY)
+    return pl.pallas_call(
+        kernel,
+        out_shape=list(outs) + [jax.ShapeDtypeStruct((1,), jnp.int32)] * flag,
+        in_specs=[in_smem] * len(smem) + [in_vmem] * len(vmem) + [in_any] * len(anywhere),
+        out_specs=[in_any if to_any else in_vmem] * len(outs) + [in_smem] * flag,
+        scratch_shapes=scratch,
+        compiler_params=pltpu.CompilerParams(vmem_limit_bytes=VMEM_BYTES),
+        cost_estimate=pl.CostEstimate(flops=flops, bytes_accessed=2 * moved, transcendentals=0),
+    )(*smem, *vmem, *anywhere)
+
+
+def body(
+    amplitudes, driver, integrals, pair_energy, col_energy, tile_irrep, pair_irrep, mirror_slot
+):
+    places, sides = lax.axis_size("virt"), lax.axis_size("pair")
+    partner_bit = sides.bit_length() - 2
+    rows, half_cols = amplitudes.shape
+    plan = Plan(2 * half_cols // TILE, integrals.shape[1] // TILE, places)
+    z, sub = lax.axis_index("virt"), lax.axis_index("sub")
+    side = (lax.axis_index("pair") >> partner_bit) & 1
+    place = jnp.stack([z, side, sub]).astype(jnp.int32)
+
+    def like(shape, dtype=integrals.dtype):
+        return jax.ShapeDtypeStruct(shape, dtype)
+
+    def over_pair(value):
+        return from_partner(value, "pair", partner_bit)
+
+    other_irrep = from_partner(tile_irrep, "sub", 0)
+    their_ints = from_partner(integrals, "sub", 0)
+    other_driver = over_pair(driver)
+
+    label_row, slot_row, energy_row = pair_irrep[None, :], mirror_slot[None, :], pair_energy[None, :]
+    lists = [pltpu.SMEM((plan.tiles,), jnp.int32), pltpu.SMEM((plan.slab * plan.tiles + 1,), jnp.int32)]
+    *sends, masked, full = call(
+        functools.partial(pack_kernel, plan),
+        (tile_irrep, other_irrep, place),
+        (integrals, their_ints, amplitudes, label_row, energy_row),
+        [like((plan.part * TILE, TILE))] * 2 + [like((rows + 16, half_cols))],
+        lists + [pltpu.SMEM((plan.tiles,), jnp.int32)],
+        flag=True,
+    )
+
+    near = plan.near
+    got = []
+    for turn in range(max(2 * (near - 1), near)):
+        pairs = []
+        for i in range(places):
+            half, at = i // near, i % near
+            if turn < 2 * (near - 1):
+                to = half * near + (at + turn // 2 + 1) % near
+                pairs.append((2 * i + half, 2 * to + half))
+            if turn < near:
+                to = (1 - half) * near + (at + turn) % near
+                pairs.append((2 * i + 1 - half, 2 * to + half))
+        got.append(lax.ppermute(sends[turn % 2], ("virt", "sub"), pairs))
+    pairs = []
+    for i in range(places):
+        for j in range(sides):
+            far = 1 - i // near
+            pairs.append(((i * sides + j) * 2 + far, (i * sides + (j ^ 1 << partner_bit)) * 2 + far))
+    swapped = [lax.ppermute(value, ("virt", "pair", "sub"), pairs) for value in got[:near]]
+
+    groups = lax.axis_size("groups")
+    ends = full
+    for apart in range(1, groups):
+        ends = jnp.maximum(
+            ends, lax.ppermute(full, "groups", [(i, (i + apart) % groups) for i in range(groups)])
+        )
+
+    cur_mine, mirror_driver, columns = call(
+        mirror_kernel,
+        (),
+        (masked, over_pair(masked), other_driver, slot_row, label_row, energy_row),
+        [like((2 * rows, half_cols)), like((rows, half_cols)), like((3 * rows, TILE), jnp.float32)],
+        anywhere=(got[0],),
+    )
+    cur_their = from_partner(cur_mine, "sub", 0)
+
+    energy = col_energy[None, :]
+    flops = 2 * 2 * rows * plan.tiles * TILE * half_cols
+    ints, cur_mine, ends = call(
+        functools.partial(first_kernel, plan, len(got)),
+        (tile_irrep, other_irrep, place, ends),
+        (integrals, their_ints, cur_mine, cur_their, driver, mirror_driver, columns, energy, *got,
+         *swapped),
+        [like((plan.tiles * TILE, half_cols)), like((2 * rows, half_cols))],
+        lists,
+        flag=True,
+        flops=flops,
+    )
+    cur_their = from_partner(cur_mine, "sub", 0)
+    (sym,) = call(
+        functools.partial(part_kernel, plan),
+        (place,),
+        (cur_mine, ints),
+        [like((rows, half_cols), jnp.float32)],
+        flops=flops // 2,
+    )
+
+    def sparse_end():
+        return call(
+            functools.partial(last_kernel, plan),
+            (tile_irrep, place),
+            (cur_their, ints, sym, driver, columns, energy),
+            [like((rows, half_cols), jnp.float32)],
+            [pltpu.VMEM((rows, half_cols), jnp.float32),
+             pltpu.SemaphoreType.DMA((plan.half // 2,))],
+            flops=flops // 2,
+            to_any=True,
+        )[0]
+
+    def dense_end():
+        return dense_plan(
+            amplitudes, driver, integrals, pair_energy, col_energy, tile_irrep, pair_irrep,
+            mirror_slot,
+        )
+
+    return lax.cond(ends[0] > 0, dense_end, sparse_end)
 
 
 def solution(mesh):

time: 180 us -> 64.1 us (0.36)
  waiting for transfers between devices: 150 us -> 27.7 us
  starting transfers between devices: 3.53 us -> 18.9 us
  Pallas kernels: 0 us -> 15.2 us
  between operations: 13.2 us -> 2.04 us
  matrix products: 9.83 us -> 0 us
  local copies, waits for them, and re-layouts: 2.18 us -> 0.04 us
    all_gather x1 -> x0, waiting for transfers between devices: 85 us -> none  [contract(): lax.all_gather(integrals, 'virt', axis=1, tiled=True)]
    ppermute x2 -> x6, waiting for transfers between devices: 44.9 us -> 25.4 us  [from_partner(): lax.ppermute(value, axis, [(i, i ^ 1 << apart) for i in range(lax.axis_si...]
    reduce_scatter x2 -> x0, waiting for transfers between devices: 18.9 us -> none  [contract(): return lax.psum_scatter(total, 'sub', scatter_dimension=1, tiled=True)]
    pallas_call x0 -> x5, Pallas kernels: none -> 15.2 us  [call(): pl.pallas_call(kernel, out_shape=list(outs) + [jax.ShapeDtypeStruct((1,),...]
    dot_general x2 -> x0, matrix products: 9.83 us -> none  [contract(): jnp.dot(blocks[0], lax.all_gather(integrals, 'virt', axis=1, tiled=True),...]
    ppermute x2 -> x6, starting transfers between devices: 3.44 us -> 12.8 us  [from_partner(): lax.ppermute(value, axis, [(i, i ^ 1 << apart) for i in range(lax.axis_si...]
    ppermute x0 -> x5, starting transfers between devices: none -> 6.05 us  [the longest x2 3.09 us: body(): got.append(lax.ppermute(sends[turn % 2], ('virt', 'sub'), pairs))]
    ppermute x0 -> x5, waiting for transfers between devices: none -> 2.27 us  [the longest x1 2.26 us: body(): lax.ppermute(full, 'groups', [(i, (i + apart) % groups) for i in range(gr...]
  transfers between devices with their start and end apart: 5 -> 11, of which waited for: 5 -> 3; matrix products, arithmetic and copies ran while one was open for 0% -> 0% of each run, Pallas kernels for 0% -> 5%
where the time goes in v3:
time: 64.1 us; the launch traced here: 63.9 us
  waiting for transfers between devices  27.7 us (43%)
  starting transfers between devices  18.9 us (29%)
  Pallas kernels  15.2 us (24%)
  between operations  2.04 us (3%)
    ppermute x6, waiting for transfers between devices, from_partner(): lax.ppermute(value, axis, [(i, i ^ 1 << apart) for i in range(lax.axis_si...  25.4 us
    pallas_call x5, Pallas kernels, call(): pl.pallas_call(kernel, out_shape=list(outs) + [jax.ShapeDtypeStruct((1,),...  15.2 us
    ppermute x6, starting transfers between devices, from_partner(): lax.ppermute(value, axis, [(i, i ^ 1 << apart) for i in range(lax.axis_si...  12.8 us
    ppermute x2, starting transfers between devices, body(): got.append(lax.ppermute(sends[turn % 2], ('virt', 'sub'), pairs))  3.09 us
    ppermute x1, waiting for transfers between devices, body(): lax.ppermute(full, 'groups', [(i, (i + apart) % groups) for i in range(gr...  2.26 us
    ppermute x1, starting transfers between devices, body(): lax.ppermute(full, 'groups', [(i, (i + apart) % groups) for i in range(gr...  1.59 us
    ppermute x2, starting transfers between devices, body(): lax.ppermute(value, ('virt', 'pair', 'sub'), pairs)  1.38 us
  transfers between devices with their start and end apart: 11, of which 3 were waited for; matrix products, arithmetic and copies ran while one was open for 0% of the time, Pallas kernels for 5%

profile of v3, /device:TPU:0, one launch (start us, length us, event | category | flops | bytes accessed | tf_op | source)
XLA Modules:
  0.0 63.9 jit_solution(9058454721642339641)
XLA Ops:
  0.0 0.5 collective-permute-start.8
  0.5 0.1 collective-permute-start.7
  0.6 0.1 pad_add_fusion.place.refs_2_
  0.7 2.3 %collective-permute-done.7.other.refs_1_ = s32[8]{0:T(128)S(1)} collective-permute-done((s32[8]{0:T(128)}, s32[8]{0:T(128)S(1)}, u32[]{:S(2)}, u32[]{:S(2)}) %collective-permute-start.7) | collective-permute-done | bytes 64 | tf_op jit(solution)/shard_map/ppermute | solution.py:16
  3.0 0.0 collective-permute-done.8.their_ref.refs_5_
  3.0 3.4 %shard_map.84 = (bf16[2048,128]{1,0:T(8,128)(2,1)S(1)}, bf16[2048,128]{1,0:T(8,128)(2,1)S(1)}, bf16[256,1024]{1,0:T(8,128)(2,1)S(1)}, s32[1]{0:T(128)}) custom-call(s32[8]{0:T(128)} %refs_0_.1, s32[8]{0:T(128)S(1)} %collective-permute-done.7.other.refs_1_, s32[3]{0:T(128)S(1)} %pad_add_fusion.place.refs_2_, bf16[1024,512]{1,0:T(8,128)(2,1)} %refs_4_.1, ...), custom_call_target="tpu_custom_call" | custom-call | bytes 5181184 | tf_op jit(solution)/shard_map/pallas_call | solution.py:295
  6.5 3.0 %collective-permute-start.12 = (bf16[2048,128]{1,0:T(8,128)(2,1)S(1)}, bf16[2048,128]{1,0:T(8,128)(2,1)S(1)}, u32[]{:S(2)}, u32[]{:S(2)}) collective-permute-start(bf16[2048,128]{1,0:T(8,128)(2,1)S(1)} %get-tuple-element.69), channel_id=1, source_target_pairs={{0,4},{1,8},{4,0},{5,12},{9,13},{8,1},{13,9},{12,5},{2,6},{3,10},{... | collective-permute-start | bytes 1572872 | tf_op jit(solution)/shard_map/ppermute | solution.py:350
  9.5 1.5 %collective-permute-start.10 = (bf16[256,1024]{1,0:T(8,128)(2,1)S(1)}, bf16[256,1024]{1,0:T(8,128)(2,1)S(1)}, u32[]{:S(2)}, u32[]{:S(2)}) collective-permute-start(bf16[256,1024]{1,0:T(8,128)(2,1)S(1)} %get-tuple-element.68.masked_ref), channel_id=1, source_target_pairs={{0,2},{2,0},{1,3},{3,1},{4,6},{6,4},{5,7},{7,5},{8,10},{10,8},{9,1... | collective-permute-start | bytes 1572872 | tf_op jit(solution)/shard_map/ppermute | solution.py:16
  11.0 0.5 collective-permute-start.11
  11.5 0.1 collective-permute-start.14
  11.6 23.1 %collective-permute-done.11.other_driver_ref = bf16[240,1024]{1,0:T(8,128)(2,1)S(1)} collective-permute-done((bf16[240,1024]{1,0:T(8,128)(2,1)}, bf16[240,1024]{1,0:T(8,128)(2,1)S(1)}, u32[]{:S(2)}, u32[]{:S(2)}) %collective-permute-start.11) | collective-permute-done | bytes 491552 | tf_op jit(solution)/shard_map/ppermute | solution.py:16
  34.7 0.0 collective-permute-done.12.after_ref.refs_12_
  34.7 0.0 collective-permute-done.10.other_masked_ref
  34.7 1.2 %shard_map.85 = (bf16[480,1024]{1,0:T(8,128)(2,1)S(1)}, bf16[240,1024]{1,0:T(8,128)(2,1)S(1)}, f32[720,128]{1,0:T(8,128)S(1)}) custom-call(bf16[256,1024]{1,0:T(8,128)(2,1)S(1)} %get-tuple-element.68.masked_ref, bf16[256,1024]{1,0:T(8,128)(2,1)S(1)} %collective-permute-done.10.other_masked_ref, ...), custom_call_target="tpu_custom_call" | custom-call | bytes 3085952 | tf_op jit(solution)/shard_map/pallas_call | solution.py:295
  35.9 0.2 collective-permute-start.13
  36.1 0.7 %collective-permute-start.15 = (bf16[2048,128]{1,0:T(8,128)(2,1)S(1)}, bf16[2048,128]{1,0:T(8,128)(2,1)S(1)}, u32[]{:S(2)}, u32[]{:S(2)}) collective-permute-start(bf16[2048,128]{1,0:T(8,128)(2,1)S(1)} %collective-permute-done.12.after_ref.refs_12_), channel_id=1, source_target_pairs={{1,3},{3,1},{5,7},{7,5},{8,10},{10,8},{12,14},{14,12},{17,19},{19,... | collective-permute-start | bytes 1572872 | tf_op jit(solution)/shard_map/ppermute | solution.py:356
  36.8 0.0 collective-permute-done.14.refs_13_
  36.8 0.7 %collective-permute-start.16 = (bf16[2048,128]{1,0:T(8,128)(2,1)S(1)}, bf16[2048,128]{1,0:T(8,128)(2,1)S(1)}, u32[]{:S(2)}, u32[]{:S(2)}) collective-permute-start(bf16[2048,128]{1,0:T(8,128)(2,1)S(1)} %collective-permute-done.14.refs_13_), channel_id=1, source_target_pairs={{1,3},{3,1},{5,7},{7,5},{8,10},{10,8},{12,14},{14,12},{17,19},{19,... | collective-permute-start | bytes 1572872 | tf_op jit(solution)/shard_map/ppermute | solution.py:356
  37.5 1.6 %collective-permute-start.9 = (s32[1]{0:T(128)}, s32[1]{0:T(128)}, u32[]{:S(2)}, u32[]{:S(2)}) collective-permute-start(s32[1]{0:T(128)} %get-tuple-element.67), channel_id=1, source_target_pairs={{0,16},{16,0},{1,17},{17,1},{2,18},{18,2},{3,19},{19,3},{4,20},{20... | collective-permute-start | bytes 20 | tf_op jit(solution)/shard_map/ppermute | solution.py:362
  39.1 2.3 %collective-permute-done.9 = s32[1]{0:T(128)} collective-permute-done((s32[1]{0:T(128)}, s32[1]{0:T(128)}, u32[]{:S(2)}, u32[]{:S(2)}) %collective-permute-start.9) | collective-permute-done | bytes 36 | tf_op jit(solution)/shard_map/ppermute | solution.py:362
  42.5 0.0 collective-permute-done.15.refs_14_
  42.5 0.0 collective-permute-done.16.refs_15_
  42.6 0.0 collective-permute-done.13.refs_7_
  42.6 5.6 %shard_map.86 = (bf16[2048,1024]{1,0:T(8,128)(2,1)S(1)}, bf16[480,1024]{1,0:T(8,128)(2,1)S(1)}, s32[1]{0:T(128)}) custom-call(s32[8]{0:T(128)S(1)} %copy-done.10, s32[8]{0:T(128)S(1)} %collective-permute-done.7.other.refs_1_, s32[3]{0:T(128)S(1)} %pad_add_fusion.place.refs_2_, s32[1]{0:T(128)S(6)} %max.3.refs_3_, bf16[1024,512]{1,0:T(8,128)(2,1)S(1)} %copy-done.2, ...), custom_call_target="tpu_custom_call" | custom-call | flops 2013265920 | bytes 15032320 | tf_op jit(solution)/shard_map/pallas_call | solution.py:295
  48.2 0.0 copy-start.8
  48.2 0.0 copy-start.9
  48.2 0.0 copy-start.11
  48.2 10.0 %collective-permute-start.17 = (bf16[480,1024]{1,0:T(8,128)(2,1)S(1)}, bf16[480,1024]{1,0:T(8,128)(2,1)S(1)}, u32[]{:S(2)}, u32[]{:S(2)}) collective-permute-start(bf16[480,1024]{1,0:T(8,128)(2,1)S(1)} %get-tuple-element.75.cur_ref), channel_id=1, source_target_pairs={{0,1},{1,0},{2,3},{3,2},{4,5},{5,4},{6,7},{7,6},{8,9},{9,8},{10,11... | collective-permute-start | bytes 2949128 | tf_op jit(solution)/shard_map/ppermute | solution.py:16
  58.9 2.3 %shard_map.87 = f32[240,1024]{1,0:T(8,128)S(1)} custom-call(s32[3]{0:T(128)S(1)} %pad_add_fusion.place.refs_2_, bf16[480,1024]{1,0:T(8,128)(2,1)S(1)} %get-tuple-element.75.cur_ref, bf16[2048,1024]{1,0:T(8,128)(2,1)S(1)} %get-tuple-element.76.ints_ref), custom_call_target="tpu_custom_call" | custom-call | flops 1006632960 | bytes 10354688 | tf_op jit(solution)/shard_map/pallas_call | solution.py:295
  61.2 0.0 collective-permute-done.17
  61.2 2.7 %conditional.1 = (f32[240,1024]{1,0:T(8,128)}) conditional(s32[]{:T(128)} %bitcast.8, (s32[8]{0:T(128)S(1)}, s32[3]{0:T(128)S(1)}, bf16[480,1024]{1,0:T(8,128)(2,1)S(1)}, bf16[2048,1024]{1,0:T(8,128)(2,1)S(1)}, f32[240,1024]{1,0:T(8,128)S(1)}, /*index=5*/bf16[240,1024]{1,0:T(8,128)(2,1)S(1)}, f32[720,128]{1,0:T(8,128)S(1)}, ...), branch_computations={%region_0.0_spmd, %region_1.3_spmd} | conditional | flops 2018430080 | bytes 100016224 | solution.py:413
  61.2 2.7 %branch_0_fun.1 = f32[240,1024]{1,0:T(8,128)} custom-call(s32[8]{0:T(128)S(1)} %get-tuple-element.40.own, s32[3]{0:T(128)S(1)} %get-tuple-element.42.place, bf16[480,1024]{1,0:T(8,128)(2,1)S(1)} %get-tuple-element.43.cur_ref, bf16[2048,1024]{1,0:T(8,128)(2,1)S(1)} %get-tuple-element.44.ints_ref, f32[240,1024]{1,0:T(8,128)S(1)} %get-tuple-element.45.sym_ref, ...), custom_call_target="tpu_custom_call" | custom-call | flops 1006632960 | bytes 14049280 | tf_op jit(solution)/shard_map/cond/branch_0_fun/pallas_call | solution.py:295
  (13 shorter events, 0.0 us)
Async XLA Ops:
  0.0 42.6 %copy-start.2 = (bf16[1024,512]{1,0:T(8,128)(2,1)S(1)}, bf16[1024,512]{1,0:T(8,128)(2,1)}, u32[]{:S(2)}) copy-start(bf16[1024,512]{1,0:T(8,128)(2,1)} %refs_4_.1) | copy-start | bytes 3145732
  0.0 42.6 %copy-start.10 = (s32[8]{0:T(128)S(1)}, s32[8]{0:T(128)}, u32[]{:S(2)}) copy-start(s32[8]{0:T(128)} %refs_0_.1) | copy-start | bytes 100
  0.0 42.6 %copy-start.3 = (bf16[240,1024]{1,0:T(8,128)(2,1)S(1)}, bf16[240,1024]{1,0:T(8,128)(2,1)}, u32[]{:S(2)}) copy-start(bf16[240,1024]{1,0:T(8,128)(2,1)} %refs_8_.1) | copy-start | bytes 1474564
  0.0 42.6 %copy-start.7 = (f32[1024]{0:T(1024)S(1)}, f32[1024]{0:T(1024)}, u32[]{:S(2)}) copy-start(f32[1024]{0:T(1024)} %param.16) | copy-start | bytes 12292
  0.0 3.0 %collective-permute-start.8 = (bf16[1024,512]{1,0:T(8,128)(2,1)}, bf16[1024,512]{1,0:T(8,128)(2,1)S(1)}, u32[]{:S(2)}, u32[]{:S(2)}) collective-permute-start(bf16[1024,512]{1,0:T(8,128)(2,1)} %refs_4_.1), channel_id=1, source_target_pairs={{0,1},{1,0},{2,3},{3,2},{4,5},{5,4},{6,7},{7,6},{8,9},{9,8},{10,11... | collective-permute-start | bytes 3145736 | tf_op jit(solution)/shard_map/ppermute | solution.py:16
  0.5 2.5 %collective-permute-start.7 = (s32[8]{0:T(128)}, s32[8]{0:T(128)S(1)}, u32[]{:S(2)}, u32[]{:S(2)}) collective-permute-start(s32[8]{0:T(128)} %refs_0_.1), channel_id=1, source_target_pairs={{0,1},{1,0},{2,3},{3,2},{4,5},{5,4},{6,7},{7,6},{8,9},{9,8},{10,11... | collective-permute-start | bytes 104 | tf_op jit(solution)/shard_map/ppermute | solution.py:16
  3.0 39.5 %copy-start = (bf16[1024,512]{1,0:T(8,128)(2,1)}, bf16[1024,512]{1,0:T(8,128)(2,1)S(1)}, u32[]{:S(2)}) copy-start(bf16[1024,512]{1,0:T(8,128)(2,1)S(1)} %collective-permute-done.8.their_ref.refs_5_) | copy-start | bytes 3145732
  6.5 28.2 %collective-permute-start.12 = (bf16[2048,128]{1,0:T(8,128)(2,1)S(1)}, bf16[2048,128]{1,0:T(8,128)(2,1)S(1)}, u32[]{:S(2)}, u32[]{:S(2)}) collective-permute-start(bf16[2048,128]{1,0:T(8,128)(2,1)S(1)} %get-tuple-element.69), channel_id=1, source_target_pairs={{0,4},{1,8},{4,0},{5,12},{9,13},{8,1},{13,9},{12,5},{2,6},{3,10},{... | collective-permute-start | bytes 1572872 | tf_op jit(solution)/shard_map/ppermute | solution.py:350
  9.5 25.2 %collective-permute-start.10 = (bf16[256,1024]{1,0:T(8,128)(2,1)S(1)}, bf16[256,1024]{1,0:T(8,128)(2,1)S(1)}, u32[]{:S(2)}, u32[]{:S(2)}) collective-permute-start(bf16[256,1024]{1,0:T(8,128)(2,1)S(1)} %get-tuple-element.68.masked_ref), channel_id=1, source_target_pairs={{0,2},{2,0},{1,3},{3,1},{4,6},{6,4},{5,7},{7,5},{8,10},{10,8},{9,1... | collective-permute-start | bytes 1572872 | tf_op jit(solution)/shard_map/ppermute | solution.py:16
  11.0 23.7 %collective-permute-start.11 = (bf16[240,1024]{1,0:T(8,128)(2,1)}, bf16[240,1024]{1,0:T(8,128)(2,1)S(1)}, u32[]{:S(2)}, u32[]{:S(2)}) collective-permute-start(bf16[240,1024]{1,0:T(8,128)(2,1)} %refs_8_.1), channel_id=1, source_target_pairs={{0,2},{2,0},{1,3},{3,1},{4,6},{6,4},{5,7},{7,5},{8,10},{10,8},{9,1... | collective-permute-start | bytes 1474568 | tf_op jit(solution)/shard_map/ppermute | solution.py:16
  11.5 25.3 %collective-permute-start.14 = (bf16[2048,128]{1,0:T(8,128)(2,1)S(1)}, bf16[2048,128]{1,0:T(8,128)(2,1)S(1)}, u32[]{:S(2)}, u32[]{:S(2)}) collective-permute-start(bf16[2048,128]{1,0:T(8,128)(2,1)S(1)} %get-tuple-element.73), channel_id=1, source_target_pairs={{0,4},{1,12},{4,0},{5,8},{9,13},{8,5},{13,9},{12,1},{2,6},{3,14},{... | collective-permute-start | bytes 1572872 | tf_op jit(solution)/shard_map/ppermute | solution.py:350
  35.9 6.7 %collective-permute-start.13 = (bf16[480,1024]{1,0:T(8,128)(2,1)S(1)}, bf16[480,1024]{1,0:T(8,128)(2,1)S(1)}, u32[]{:S(2)}, u32[]{:S(2)}) collective-permute-start(bf16[480,1024]{1,0:T(8,128)(2,1)S(1)} %get-tuple-element.70.refs_6_), channel_id=1, source_target_pairs={{0,1},{1,0},{2,3},{3,2},{4,5},{5,4},{6,7},{7,6},{8,9},{9,8},{10,11... | collective-permute-start | bytes 2949128 | tf_op jit(solution)/shard_map/ppermute | solution.py:16
  36.1 6.4 %collective-permute-start.15 = (bf16[2048,128]{1,0:T(8,128)(2,1)S(1)}, bf16[2048,128]{1,0:T(8,128)(2,1)S(1)}, u32[]{:S(2)}, u32[]{:S(2)}) collective-permute-start(bf16[2048,128]{1,0:T(8,128)(2,1)S(1)} %collective-permute-done.12.after_ref.refs_12_), channel_id=1, source_target_pairs={{1,3},{3,1},{5,7},{7,5},{8,10},{10,8},{12,14},{14,12},{17,19},{19,... | collective-permute-start | bytes 1572872 | tf_op jit(solution)/shard_map/ppermute | solution.py:356
  36.8 5.8 %collective-permute-start.16 = (bf16[2048,128]{1,0:T(8,128)(2,1)S(1)}, bf16[2048,128]{1,0:T(8,128)(2,1)S(1)}, u32[]{:S(2)}, u32[]{:S(2)}) collective-permute-start(bf16[2048,128]{1,0:T(8,128)(2,1)S(1)} %collective-permute-done.14.refs_13_), channel_id=1, source_target_pairs={{1,3},{3,1},{5,7},{7,5},{8,10},{10,8},{12,14},{14,12},{17,19},{19,... | collective-permute-start | bytes 1572872 | tf_op jit(solution)/shard_map/ppermute | solution.py:356
  37.5 3.8 %collective-permute-start.9 = (s32[1]{0:T(128)}, s32[1]{0:T(128)}, u32[]{:S(2)}, u32[]{:S(2)}) collective-permute-start(s32[1]{0:T(128)} %get-tuple-element.67), channel_id=1, source_target_pairs={{0,16},{16,0},{1,17},{17,1},{2,18},{18,2},{3,19},{19,3},{4,20},{20... | collective-permute-start | bytes 20 | tf_op jit(solution)/shard_map/ppermute | solution.py:362
  48.2 13.0 %copy-start.8 = (s32[240]{0:T(256)S(1)}, s32[240]{0:T(256)}, u32[]{:S(2)}) copy-start(s32[240]{0:T(256)} %param.18) | copy-start | bytes 2884
  48.2 13.0 %copy-start.9 = (f32[240]{0:T(256)S(1)}, f32[240]{0:T(256)}, u32[]{:S(2)}) copy-start(f32[240]{0:T(256)} %param.15) | copy-start | bytes 2884
  48.2 13.0 %copy-start.11 = (s32[240]{0:T(256)S(1)}, s32[240]{0:T(256)}, u32[]{:S(2)}) copy-start(s32[240]{0:T(256)} %param.19) | copy-start | bytes 2884
  48.2 12.9 %collective-permute-start.17 = (bf16[480,1024]{1,0:T(8,128)(2,1)S(1)}, bf16[480,1024]{1,0:T(8,128)(2,1)S(1)}, u32[]{:S(2)}, u32[]{:S(2)}) collective-permute-start(bf16[480,1024]{1,0:T(8,128)(2,1)S(1)} %get-tuple-element.75.cur_ref), channel_id=1, source_target_pairs={{0,1},{1,0},{2,3},{3,2},{4,5},{5,4},{6,7},{7,6},{8,9},{9,8},{10,11... | collective-permute-start | bytes 2949128 | tf_op jit(solution)/shard_map/ppermute | solution.py:16
